TPU v7x, 256 devices: a whole 4x4x8 slice. The times are simulated.
256 devices in a mesh: gx: 8 (over x, core), gy: 32 (over y, z).
Axes of the slice: x: 4, y: 4, z: 8, core: 2. Of those that a mesh axis runs over, the one named last changes fastest.
Arguments:
- rock_rhs: float32 [256, 512, 128], P('gx', 'gy'), may hold values from -6 to 6
- frac_rhs: float32 [8192, 4096], P(('gx', 'gy')), may hold values from -6 to 6
- perm: float32 [256, 512, 128], P('gx', 'gy'), may hold values from 0.1 to 10
- storage: float32 [256, 512, 128], P('gx', 'gy'), may hold values from 0.002 to 0.05
- pressure: float32 [256, 512, 128], P('gx', 'gy'), may hold values from -4 to 4
- frac_perm: float32 [8192, 4096], P(('gx', 'gy')), may hold values from 0.5 to 20
- frac_storage: float32 [8192, 4096], P(('gx', 'gy')), may hold values from 0.002 to 0.05
- frac_pressure: float32 [8192, 4096], P(('gx', 'gy')), may hold values from -4 to 4
- couple_geom: float32 [8192, 128], P(('gx', 'gy')), may hold values from 0.1 to 2
- couple_count: int32 [8192], P(('gx', 'gy')), may hold values from 1 to 128, as said below
- couple_frac_cell: int32 [8192, 128], P(('gx', 'gy')), may hold values from 0 to 4095
- couple_rock_cell: int32 [8192, 128], P(('gx', 'gy')), may hold values from 0 to 65535
- host_offset: int32 [8192], P(('gx', 'gy')), may hold values from -1 to 1, as said below
- cross_pairs: int32 [2, 65536], P(None, ('gx', 'gy')), may hold values from 0 to 131071, as said below
- cross_geom: float32 [65536], P(('gx', 'gy')), may hold values from 0.1 to 2
- aggregates: int32 [256, 512, 128], P('gx', 'gy'), may hold values from 0 to 63, as said below
Outputs:
- rock_update: float32 [256, 512, 128], P('gx', 'gy')
- frac_update: float32 [8192, 4096], P(('gx', 'gy'))
- residual_norm: float32 [], replicated
Inputs may be any that keep to these rules, and one draw needn't show every extreme that they name: `couple_count`: every fracture has at least one live slot, and in every draw some fracture fills all 128. `host_offset`: the host block always exists: owners at the first gy index never have -1, owners at the last never +1. `cross_pairs`: cells are numbered within the owner device's 32 fractures, 4096 each; the two ends of a pair lie in different fractures. `aggregates`: each aggregate is a face-connected set of cells inside one device's block; every one of the 64 numbers is used in every block, with counts that differ from block to block.
All inputs are finite; a program needn't handle non-finite values.
Results may differ from a plain program's by a relative error of at most 0.0003.
Values sent between devices are 32-bit elements; how exact they have to be, the bound alone decides.
A program may use at most 128 MiB of HBM per device.

v0:
```python
import functools

import jax
import jax.numpy as jnp
from jax import lax
from jax.experimental import pallas as pl
from jax.experimental.pallas import tpu as pltpu
from jax.sharding import PartitionSpec as P

CX, CY, NZ = 32, 16, 128
FR, FCELLS, FSIDE, KC = 32, 4096, 64, 128
SLABS = FCELLS // 128
NAGG = 64
ROWS = CX * CY
CROSS = 256
relaxation = 0.8
epsilon = 1e-06
MESH = pl.DeviceIdType.MESH
f32 = jnp.float32
bf16 = jnp.bfloat16


def iota(shape, dim):
    return lax.broadcasted_iota(jnp.int32, shape, dim)


def loop(count, body, unroll=1):
    lax.fori_loop(0, count, lambda i, c: (body(i), c)[1], 0, unroll=unroll)


def halves(x):
    high = x.astype(bf16)
    return high, (x - high.astype(f32)).astype(bf16)


def nt_dot(a, b):
    return lax.dot_general(a, b, (((1,), (1,)), ((), ())), preferred_element_type=f32)


def lanes_of(table, index):
    return jnp.take_along_axis(table, index, axis=1)


def kernel(
    sizes,
    rock_rhs, frac_rhs, perm, storage, pressure, frac_perm, frac_storage, frac_pressure,
    geom, count, frac_cell, rock_cell, offset, pairs, cross_geom, agg,
    rock_out, frac_out, res_out,
    Z0, E, PA, PE, WX, WYM, WYP, WZM, WZP, RD, INVR, W1R, Q, S, DEL, SEG,
    FD, INVF, TAP, TAM, TCP, TCM, W1F, ZF, F2, S2,
    U, LV, BF, XU, LVX, XV, IDX, OFF, CPL, PICK, HV, AGS, VALS,
    sx, rx, sy, ry, sic, ric, sag, rag, szy, rzy, sfl, rfl, sans, rans, scs, rcs,
    AR0, AR1, AR2, send_sem, recv_sem,
):
    n_gx, n_y, n_z = sizes
    n_gy = n_y * n_z
    gx = lax.axis_index("gx")
    gy = lax.axis_index("gy")
    my_y, my_z = gy // n_z, gy % n_z
    x_dev = [((gx + 1) % n_gx, gy), ((gx + n_gx - 1) % n_gx, gy)]
    y_dev = [(gx, (gy + 1) % n_gy), (gx, (gy + n_gy - 1) % n_gy)]
    gx_peers = [((gx + p) % n_gx, gy) for p in range(1, n_gx)]
    y_peers = [(gx, (my_y + p) % n_y * n_z + my_z) for p in range(1, n_y)]
    z_peers = [(gx, my_y * n_z + (my_z + p) % n_z) for p in range(1, n_z)]

    barrier = pltpu.get_barrier_semaphore()
    everyone = gx_peers + y_peers + z_peers + y_dev
    for device in everyone:
        pl.semaphore_signal(barrier, inc=1, device_id=device, device_id_type=MESH)

    started = []

    def send(src, dst, device):
        number = len(started)
        copy = pltpu.make_async_remote_copy(
            src_ref=src, dst_ref=dst, send_sem=send_sem.at[number],
            recv_sem=recv_sem.at[number], device_id=device, device_id_type=MESH,
        )
        copy.start()
        started.append(copy)
        return copy

    sub8 = iota((8, 128), 0)
    sub16 = iota((16, 128), 0)
    sub32 = iota((32, 128), 0)
    sub128 = iota((128, 128), 0)
    lane16 = iota((16, 128), 1)
    lane32 = iota((32, 128), 1)
    row_lane = iota((1, 128), 1)

    def to_table(get):
        def body(r):
            F2[pl.ds(r, FR, stride=SLABS), :] = get(r)
        loop(SLABS, body, 2)

    def slab(r):
        return pl.ds(pl.multiple_of(r * 128, 128), 128)

    def pick_slots(out):
        def body(f):
            cell = frac_cell[pl.ds(f, 1), :]
            table = F2[pl.ds(pl.multiple_of(f * SLABS, SLABS), SLABS), :]
            got = lanes_of(table, jnp.broadcast_to(cell & 127, (SLABS, 128)))
            out[pl.ds(f, 1), :] = jnp.sum(
                jnp.where(sub32 == cell >> 7, got, 0.0), axis=0, keepdims=True)
        loop(FR, body, 4)

    ends = [(e, h) for e in (0, 1) for h in (0, 1)]

    def end_cells(e, h):
        return pairs[e : e + 1, h * 128 : (h + 1) * 128]

    def pick_ends():
        low = [jnp.broadcast_to(end_cells(e, h) & 127, (8, 128)) for e, h in ends]
        high = [(end_cells(e, h) >> 7) - sub8 for e, h in ends]

        def body(i, accs):
            for j in range(4):
                row = pl.multiple_of(i * 32 + j * 8, 8)
                table = F2[pl.ds(row, 8), :]
                accs = tuple(
                    jnp.where(high[n] == row, lanes_of(table, low[n]), accs[n])
                    for n in range(4)
                )
            return accs
        accs = lax.fori_loop(0, FR * SLABS // 32, body, (jnp.zeros((8, 128), f32),) * 4)
        return [jnp.sum(a, axis=0, keepdims=True) for a in accs]

    def spread_frac(slot_vals, end_vals):
        for n, (e, h) in enumerate(ends):
            hot = sub128 == (end_cells(e, h) & 127)
            high, low = halves(end_vals[n])
            LVX[0:128, n * 128 : (n + 1) * 128] = jnp.where(hot, high.astype(f32), 0.0).astype(bf16)
            LVX[128:256, n * 128 : (n + 1) * 128] = jnp.where(hot, low.astype(f32), 0.0).astype(bf16)
        for m in range(4):
            part = nt_dot(XU[m * 256 : (m + 1) * 256, :], LVX[...])
            S2[m * 256 : (m + 1) * 256, :] = part[:, :128] + part[:, 128:]

        def body(f):
            cell = frac_cell[pl.ds(f, 1), :]
            high, low = halves(jnp.where(sub32 == cell >> 7, slot_vals[pl.ds(f, 1), :], 0.0))
            part = nt_dot(jnp.concatenate([high, low], axis=0), BF[f])
            rows = pl.ds(pl.multiple_of(f * SLABS, SLABS), SLABS)
            S2[rows, :] = S2[rows, :] + part[:32] + part[32:]
        loop(FR, body, 2)

    def build_hot(src):
        def body(f):
            high = IDX[src, pl.ds(f, 1), :] >> 7
            for m in range(4):
                hot = (sub128 + m * 128 == high).astype(f32).astype(bf16)
                U[src, m * 128 : (m + 1) * 128, slab(f)] = hot
        loop(FR, body)

    def spread_rock(src, vals, first):
        def body(f):
            hot = sub128 == (IDX[src, pl.ds(f, 1), :] & 127)
            high, low = halves(vals[pl.ds(f, 1), :])
            LV[0:128, slab(f)] = jnp.where(hot, high.astype(f32), 0.0).astype(bf16)
            LV[128:256, slab(f)] = jnp.where(hot, low.astype(f32), 0.0).astype(bf16)
        loop(FR, body, 2)
        for m in range(2):
            part = nt_dot(U[src, m * 256 : (m + 1) * 256, :], LV[...])
            total = part[:, :128] + part[:, 128:]
            rows = pl.ds(m * 256, 256)
            DEL[rows, :] = total if first else DEL[rows, :] + total

    def pick_rock(get, outs):
        def body(f):
            cells = [IDX[src, pl.ds(f, 1), :] for src in range(3)]
            low = [jnp.broadcast_to(c & 127, (8, 128)) for c in cells]
            high = [(c >> 7) - sub8 for c in cells]
            accs = [jnp.zeros((8, 128), f32)] * 3
            for i in range(CX):
                for j in range(2):
                    table = get(i, j)
                    row = i * 16 + j * 8
                    accs = [
                        jnp.where(high[n] == row, lanes_of(table, low[n]), accs[n])
                        for n in range(3)
                    ]
            for n in range(3):
                outs[n][pl.ds(f, 1), :] = jnp.sum(accs[n], axis=0, keepdims=True)
        loop(FR, body)

    def aggregate_sums(src):
        for chunk in range(4):
            def body(i, accs):
                for j in (0, 8):
                    value, number = src[i, j : j + 8, :], agg[i, j : j + 8, :]
                    accs = tuple(
                        acc + jnp.where(number == chunk * 16 + a, value, 0.0)
                        for a, acc in enumerate(accs)
                    )
                return accs
            accs = lax.fori_loop(0, CX, body, (jnp.zeros((8, 128), f32),) * 16)
            for a, acc in enumerate(accs):
                SEG[chunk * 16 + a : chunk * 16 + a + 1, :] = jnp.sum(acc, axis=0, keepdims=True)
        ones = jnp.ones((16, 128), bf16)
        rest = SEG[...]
        total = jnp.zeros((16, 128), f32)
        for _ in range(3):
            high = rest.astype(bf16)
            rest = rest - high.astype(f32)
            total = total + nt_dot(ones, high)
        return total

    SEG[NAGG:128, :] = jnp.zeros((128 - NAGG, 128), f32)

    to_table(lambda r: frac_pressure[:, slab(r)])
    pick_slots(PICK)

    def split_slots(f):
        where = offset[f]
        row = pl.ds(f, 1)
        OFF[row, :] = jnp.full((1, 128), where, jnp.int32)
        cell = rock_cell[row, :]
        live = row_lane < count[f]
        IDX[0, row, :] = jnp.where(live & (where == 0), cell, -1)
        sic[0, 0, row, :] = jnp.where(live & (where == 1), cell, -1).astype(f32)
        sic[1, 0, row, :] = jnp.where(live & (where == -1), cell, -1).astype(f32)
        value = jnp.where(live, geom[row, :] * jnp.exp(-0.5 * PICK[row, :]), 0.0)
        CPL[row, :] = value
    loop(FR, split_slots, 2)
    sic[0, 1] = CPL[...]
    sic[1, 1] = CPL[...]

    for d, plane in enumerate((CX - 1, 0)):
        sx[d, 0] = perm[plane]
        sx[d, 1] = pressure[plane]
        sx[d, 2] = agg[plane].astype(f32)
    for d, row in enumerate((CY - 1, 0)):
        sy[d, 0] = perm[:, row, :]
        sy[d, 1] = pressure[:, row, :]
        sy[d, 2] = agg[:, row, :].astype(f32)

    pl.semaphore_wait(barrier, len(everyone))
    slots_sent = [send(sic.at[d], ric.at[d], y_dev[d]) for d in (0, 1)]
    faces_sent = [send(sx.at[d], rx.at[d], x_dev[d]) for d in (0, 1)]
    faces_sent += [send(sy.at[d], ry.at[d], y_dev[d]) for d in (0, 1)]

    def face_along(r):
        conduct, press = frac_perm[:, slab(r)], frac_pressure[:, slab(r)]
        scaled = conduct * jnp.exp(-0.25 * press)
        F2[pl.ds(r, FR, stride=SLABS), :] = press
        near, near_scaled = pltpu.roll(conduct, 127, 1), pltpu.roll(scaled, 127, 1)
        weight = 2.0 * scaled * near_scaled / (conduct + near)
        weight = jnp.where(lane32 % FSIDE < FSIDE - 1, weight, 0.0)
        TAP[:, slab(r)] = weight
        TAM[:, slab(r)] = pltpu.roll(weight, 1, 1)
        after = slab(jnp.minimum(r + 1, SLABS - 1))
        next_conduct = frac_perm[:, after]
        next_scaled = next_conduct * jnp.exp(-0.25 * frac_pressure[:, after])
        first = lane32 < FSIDE
        near = pltpu.roll(jnp.where(first, next_conduct, conduct), FSIDE, 1)
        near_scaled = pltpu.roll(jnp.where(first, next_scaled, scaled), FSIDE, 1)
        weight = 2.0 * scaled * near_scaled / (conduct + near)
        TCP[:, slab(r)] = jnp.where(first | (r < SLABS - 1), weight, 0.0)
    loop(SLABS, face_along)

    pressures = pick_ends()
    for n, (e, h) in enumerate(ends):
        for m in range(8):
            hot = (sub128 + m * 128 == end_cells(e, h) >> 7).astype(f32).astype(bf16)
            XU[m * 128 : (m + 1) * 128, n * 128 : (n + 1) * 128] = hot
    for h in (0, 1):
        XV[h : h + 1, :] = cross_geom[0:1, h * 128 : (h + 1) * 128] * jnp.exp(
            -0.25 * (pressures[h] + pressures[h + 2]))

    def build_lanes(f):
        BF[f] = (sub128 == (frac_cell[pl.ds(f, 1), :] & 127)).astype(f32).astype(bf16)
    loop(FR, build_lanes)
    coefs = [XV[h : h + 1, :] for h in (0, 1)]
    spread_frac(CPL, coefs + coefs)

    def face_back(r):
        before = slab(jnp.maximum(r - 1, 0))
        first = lane32 < FSIDE
        own = TCP[:, slab(r)]
        back = pltpu.roll(jnp.where(first, own, TCP[:, before]), FSIDE, 1)
        back = jnp.where(jnp.logical_not(first) | (r > 0), back, 0.0)
        TCM[:, slab(r)] = back
        diag = frac_storage[:, slab(r)] + TAP[:, slab(r)] + TAM[:, slab(r)] + own + back
        diag = diag + S2[pl.ds(r, FR, stride=SLABS), :]
        FD[:, slab(r)] = diag
        INVF[:, slab(r)] = relaxation / diag
    loop(SLABS, face_back)

    def smooth_frac(k, source):
        def body(r):
            z = source[:, slab(r)] * INVF[:, slab(r)]
            ZF[k, :, slab(r)] = z
            F2[pl.ds(r, FR, stride=SLABS), :] = z
        loop(SLABS, body, 2)
        pick_slots(PICK)
        sfl[k] = CPL[...] * PICK[...]
        return [send(sfl.at[k], rfl.at[k, d], y_dev[d]) for d in (0, 1)]

    flux_sent = smooth_frac(0, frac_rhs)

    build_hot(0)
    spread_rock(0, CPL, True)
    for copy in slots_sent:
        copy.wait_recv()
    for d in (0, 1):
        IDX[1 + d] = ric[d, 0].astype(jnp.int32)
        build_hot(1 + d)
        spread_rock(1 + d, ric.at[d, 1], False)
    pick_rock(lambda i, j: agg[i, j * 8 : j * 8 + 8, :].astype(f32), [AGS, sag.at[0], sag.at[1]])
    aggs_sent = [send(sag.at[1 - d], rag.at[d], y_dev[d]) for d in (0, 1)]

    for copy in faces_sent:
        copy.wait_recv()
    open_x = [gx > 0, gx < n_gx - 1]
    open_y = [gy > 0, gy < n_gy - 1]

    def scale_rock(i):
        conduct = perm[i]
        PA[i + 1] = conduct
        PE[i + 1] = conduct * jnp.exp(-0.25 * pressure[i])
    loop(CX, scale_rock)
    for d, plane in enumerate((0, CX + 1)):
        conduct = jnp.where(open_x[d], rx[d, 0], 0.0)
        PA[plane] = conduct
        PE[plane] = conduct * jnp.exp(-0.25 * rx[d, 1])
    for d in (0, 1):
        conduct = jnp.where(open_y[d], ry[d, 0], 0.0)
        ry[d, 0] = conduct
        ry[d, 1] = conduct * jnp.exp(-0.25 * ry[d, 1])

    def below(x, edge):
        return jnp.where(sub16 == 0, edge, pltpu.roll(x, 1, 0))

    def above(x, edge):
        return jnp.where(sub16 == CY - 1, edge, pltpu.roll(x, CY - 1, 0))

    def rock_faces(i):
        conduct, scaled = PA[i + 1], PE[i + 1]
        row = pl.ds(i, 1)

        def weight(near, near_scaled):
            return 2.0 * scaled * near_scaled / (conduct + near)
        WX[i] = weight(PA[i], PE[i])
        WYM[i] = weight(below(conduct, ry[0, 0, row, :]), below(scaled, ry[0, 1, row, :]))
        WYP[i] = weight(above(conduct, ry[1, 0, row, :]), above(scaled, ry[1, 1, row, :]))
        up = weight(pltpu.roll(conduct, 127, 1), pltpu.roll(scaled, 127, 1))
        up = jnp.where(lane16 < NZ - 1, up, 0.0)
        WZP[i] = up
        WZM[i] = pltpu.roll(up, 1, 1)
    loop(CX, rock_faces)
    WX[CX] = 2.0 * PE[CX] * PE[CX + 1] / (PA[CX] + PA[CX + 1])

    def rock_diagonal(i):
        faces = [WX[i], WX[i + 1], WYM[i], WYP[i], WZM[i], WZP[i]]
        rows = pl.ds(pl.multiple_of(i * CY, CY), CY)
        diag = storage[i] + sum(faces) + DEL[rows, :]
        RD[i] = diag
        INVR[i] = relaxation / diag
        mine = agg[i]
        inside = lambda n: jnp.clip(n, 0, CX - 1)
        nears = [
            jnp.where(i > 0, agg[inside(i - 1)], -1),
            jnp.where(i < CX - 1, agg[inside(i + 1)], -1),
            below(mine, -1), above(mine, -1),
            pltpu.roll(mine, 1, 1), pltpu.roll(mine, 127, 1),
        ]
        for face, near in zip(faces, nears):
            diag = diag - jnp.where(near == mine, face, 0.0)
        S[i] = diag
    loop(CX, rock_diagonal)
    coarse_diag = aggregate_sums(S)
    coarse_diag = jnp.where(lane16 < NAGG, coarse_diag, 1.0)

    def stencil(i, center, low_x, high_x, low_y, high_y):
        out = RD[i] * center
        out = out - WX[i] * low_x - WX[i + 1] * high_x
        out = out - WYM[i] * below(center, low_y) - WYP[i] * above(center, high_y)
        return out - WZM[i] * pltpu.roll(center, 1, 1) - WZP[i] * pltpu.roll(center, 127, 1)

    def iterate(k, rock_vec, frac_vec, flux_sent):
        def smooth_rock(i):
            Z0[k, i + 1] = rock_vec[i] * INVR[i]
        loop(CX, smooth_rock, 2)
        for d, row in enumerate((CY - 1, 0)):
            szy[k, d] = Z0[k, 1 : CX + 1, row, :]
        halo_sent = [
            send(Z0.at[k, CX], Z0.at[k, 0], x_dev[0]),
            send(Z0.at[k, 1], Z0.at[k, CX + 1], x_dev[1]),
        ] + [send(szy.at[k, d], rzy.at[k, d], y_dev[d]) for d in (0, 1)]
        pick_rock(lambda i, j: Z0[k, i + 1, j * 8 : j * 8 + 8, :],
                  [HV, sans.at[k, 0], sans.at[k, 1]])
        answers_sent = [send(sans.at[k, 1 - d], rans.at[k, d], y_dev[d]) for d in (0, 1)]
        values = pick_ends()
        spread_rock(0, sfl.at[k], True)
        for d, copy in enumerate(flux_sent):
            copy.wait_recv()
            spread_rock(1 + d, rfl.at[k, d], False)
        for copy in halo_sent:
            copy.wait_recv()

        def residual(i):
            row = pl.ds(i, 1)
            rows = pl.ds(pl.multiple_of(i * CY, CY), CY)
            image = stencil(i, Z0[k, i + 1], Z0[k, i], Z0[k, i + 2],
                            rzy[k, 0, row, :], rzy[k, 1, row, :]) - DEL[rows, :]
            Q[i] = image
            S[i] = rock_vec[i] - image
        loop(CX, residual)
        coarse = aggregate_sums(S) / coarse_diag
        scs[k] = coarse[0:8]
        coarse_sent = [send(scs.at[k], rcs.at[k, d], x_dev[d]) for d in (0, 1)]
        coarse_sent += [send(scs.at[k], rcs.at[k, 2 + d], y_dev[d]) for d in (0, 1)]

        def correct(i):
            E[k, i + 1] = lanes_of(coarse, agg[i])
        loop(CX, correct, 2)
        if k == 0:
            for copy in aggs_sent:
                copy.wait_recv()
            AGS[...] = AGS[...] + rag[0] + rag[1]
        for copy in answers_sent + coarse_sent:
            copy.wait_recv()
        tables = [jnp.concatenate([rcs[k, d], rcs[k, d]], axis=0) for d in range(4)]
        for d, plane in enumerate((0, CX + 1)):
            E[k, plane] = lanes_of(tables[d], rx[d, 2].astype(jnp.int32))
        for d in (0, 1):
            table = jnp.concatenate([tables[2 + d]] * 2, axis=0)
            VALS[d] = lanes_of(table, ry[d, 2].astype(jnp.int32))
        slot_agg = AGS[...].astype(jnp.int32)
        four = [jnp.concatenate([t] * 2, axis=0) for t in (coarse, tables[2], tables[3])]
        own, low, high = [lanes_of(t, slot_agg) for t in four]
        where = OFF[...]
        host = HV[...] + rans[k, 0] + rans[k, 1]
        host = host + jnp.where(where == 0, own, jnp.where(where < 0, low, high))
        VALS[2] = CPL[...] * host
        coefs = [XV[h : h + 1, :] for h in (0, 1)]
        spread_frac(VALS.at[2], [coefs[h] * values[2 * (1 - e) + h] for e, h in ends])

        zero = jnp.zeros((8, 128), f32)

        def fold(x):
            return sum(x[j : j + 8] for j in range(0, x.shape[0], 8))

        def products(x, v, b):
            if k == 0:
                return fold(v * v), fold(x * v), fold(x * x)
            return fold(x * b), fold(x * v), fold(x * x)

        def rock_image(i, accs):
            row = pl.ds(i, 1)
            vec = rock_vec[i]
            image = Q[i] + stencil(i, E[k, i + 1], E[k, i], E[k, i + 2],
                                   VALS[0, row, :], VALS[1, row, :])
            image = image - relaxation * vec
            if k == 0:
                W1R[i] = image
            return tuple(a + p for a, p in zip(accs, products(image, vec, rock_rhs[i])))
        accs = lax.fori_loop(0, CX, rock_image, (zero,) * 3)

        def frac_image(r, accs):
            here = slab(r)
            vec = frac_vec[:, here]
            z = ZF[k, :, here]
            before = ZF[k, :, slab(jnp.maximum(r - 1, 0))]
            after = ZF[k, :, slab(jnp.minimum(r + 1, SLABS - 1))]
            first = lane32 < FSIDE
            down = pltpu.roll(jnp.where(first, after, z), FSIDE, 1)
            up = pltpu.roll(jnp.where(first, z, before), FSIDE, 1)
            image = FD[:, here] * z - S2[pl.ds(r, FR, stride=SLABS), :]
            image = image - TAP[:, here] * pltpu.roll(z, 127, 1) - TAM[:, here] * pltpu.roll(z, 1, 1)
            image = image - TCP[:, here] * down - TCM[:, here] * up
            image = image - relaxation * vec
            if k == 0:
                W1F[:, here] = image
            return tuple(a + p for a, p in zip(accs, products(image, vec, frac_rhs[:, here])))
        return lax.fori_loop(0, SLABS, frac_image, accs)

    dots = list(iterate(0, rock_rhs, frac_rhs, flux_sent))
    flux_sent = smooth_frac(1, W1F)
    dots += list(iterate(1, W1R, W1F, flux_sent))

    tile = jnp.zeros((8, 128), f32)
    for n, part in enumerate(dots):
        tile = jnp.where(sub8 == n, jnp.sum(part, axis=0, keepdims=True), tile)
    groups = [(AR0, gx, gx_peers, n_gx), (AR1, my_y, y_peers, n_y), (AR2, my_z, z_peers, n_z)]
    for slots, me, peers, size in groups:
        slots[pl.ds(me, 1)] = tile[None]
        copies = [send(slots.at[me], slots.at[me], device) for device in peers]
        for copy in copies:
            copy.wait_recv()
        tile = sum(slots[n] for n in range(size))
    tile = jnp.sum(tile, axis=1, keepdims=True)
    bb, pb, pp, qb, qp, qq = [tile[n : n + 1, :] for n in range(6)]
    gram = [[bb, pb, qb], [pb, pp, qp], [qb, qp, qq]]
    shift = relaxation

    def inner(a, c):
        return sum(a[m] * c[n] * gram[m][n] for m in range(3) for n in range(3))

    one, none = jnp.ones((1, 1), f32), jnp.zeros((1, 1), f32)
    start_norm = jnp.sqrt(bb + epsilon)
    v0 = [one / start_norm, none, none]
    image = [shift * v0[0], v0[0], none]
    rest0 = inner(image, image)
    h00 = inner(image, v0)
    image = [a - h00 * c for a, c in zip(image, v0)]
    h10 = jnp.sqrt(jnp.maximum(inner(image, image), 0.0) + epsilon)
    v1 = [a / h10 for a in image]
    image = [shift * v1[0], v1[0] + shift * v1[1], v1[1]]
    h01, h11 = inner(image, v0), inner(image, v1)
    image = [a - h01 * c - h11 * d for a, c, d in zip(image, v0, v1)]
    h21 = jnp.sqrt(jnp.maximum(inner(image, image), 0.0) + epsilon)

    radius = jnp.sqrt(h00 * h00 + h10 * h10)
    cosine, sine = h00 / radius, h10 / radius
    upper01 = cosine * h01 + sine * h11
    lower = cosine * h11 - sine * h01
    right0, right1 = cosine * start_norm, -sine * start_norm
    radius1 = jnp.sqrt(lower * lower + h21 * h21)
    cosine1, sine1 = lower / radius1, h21 / radius1
    res_out[...] = jnp.abs(-sine1 * right1)
    y1 = cosine1 * right1 / radius1
    y0 = (right0 - upper01 * y1) / radius
    on_b = y0 * v0[0] + y1 * v1[0]
    on_p = y1 * v1[1]

    def rock_update(i):
        rock_out[i] = on_b * (Z0[0, i + 1] + E[0, i + 1]) + on_p * (Z0[1, i + 1] + E[1, i + 1])
    loop(CX, rock_update, 2)

    def frac_update(r):
        frac_out[:, slab(r)] = on_b * ZF[0, :, slab(r)] + on_p * ZF[1, :, slab(r)]
    loop(SLABS, frac_update, 2)
    for copy in started:
        copy.wait_send()


def local(sizes, rock_rhs, frac_rhs, perm, storage, pressure, frac_perm, frac_storage,
          frac_pressure, couple_geom, couple_count, couple_frac_cell, couple_rock_cell,
          host_offset, cross_pairs, cross_geom, aggregates):
    n_gx, n_y, n_z = sizes
    vmem = pl.BlockSpec(memory_space=pltpu.VMEM)
    smem = pl.BlockSpec(memory_space=pltpu.SMEM)
    in_specs = [vmem] * 16
    in_specs[9] = in_specs[12] = smem
    block = (CX, CY, NZ)
    tall = (CX + 2, CY, NZ)
    frac = (FR, FCELLS)
    slot = (FR, KC)

    def mem(*shape, kind=f32):
        return pltpu.VMEM(shape, kind)

    scratch = [
        mem(2, *tall), mem(2, *tall), mem(*tall), mem(*tall), mem(CX + 1, CY, NZ),
        *[mem(*block) for _ in range(9)], mem(ROWS, 128), mem(128, 128),
        *[mem(*frac) for _ in range(7)], mem(2, *frac), mem(FR * SLABS, 128), mem(FR * SLABS, 128),
        mem(3, ROWS, FR * KC, kind=bf16), mem(256, FR * KC, kind=bf16),
        mem(FR, 128, 128, kind=bf16), mem(FR * SLABS, 2 * CROSS, kind=bf16),
        mem(256, 2 * CROSS, kind=bf16), mem(8, 128),
        mem(3, *slot, kind=jnp.int32), mem(*slot, kind=jnp.int32),
        mem(*slot), mem(*slot), mem(*slot), mem(*slot), mem(3, *slot),
        mem(2, 3, CY, NZ), mem(2, 3, CY, NZ), mem(2, 3, CX, NZ), mem(2, 3, CX, NZ),
        mem(2, 2, *slot), mem(2, 2, *slot), mem(2, *slot), mem(2, *slot),
        mem(2, 2, CX, NZ), mem(2, 2, CX, NZ), mem(2, *slot), mem(2, 2, *slot),
        mem(2, 2, *slot), mem(2, 2, *slot), mem(2, 8, 128), mem(2, 4, 8, 128),
        mem(n_gx, 8, 128), mem(n_y, 8, 128), mem(n_z, 8, 128),
        pltpu.SemaphoreType.DMA((64,)), pltpu.SemaphoreType.DMA((64,)),
    ]
    rock, fracs, norm = pl.pallas_call(
        functools.partial(kernel, sizes),
        out_shape=(
            jax.ShapeDtypeStruct(block, f32),
            jax.ShapeDtypeStruct(frac, f32),
            jax.ShapeDtypeStruct((1, 1), f32),
        ),
        in_specs=in_specs,
        out_specs=(vmem, vmem, vmem),
        scratch_shapes=scratch,
        compiler_params=pltpu.CompilerParams(
            collective_id=0, has_side_effects=True, vmem_limit_bytes=60 * 1024 * 1024),
    )(rock_rhs, frac_rhs, perm, storage, pressure, frac_perm, frac_storage, frac_pressure,
      couple_geom, couple_count, couple_frac_cell, couple_rock_cell, host_offset, cross_pairs,
      cross_geom.reshape(1, CROSS), aggregates)
    return rock, fracs, norm[0, 0]


def solution(mesh):
    n_gx, n_gy = mesh.shape["gx"], mesh.shape["gy"]
    n_z = 8 if n_gy % 8 == 0 else 2
    grid = P("gx", "gy", None)
    owned = P(("gx", "gy"), None)
    flat = P(("gx", "gy"))
    in_specs = (grid, owned, grid, grid, grid, owned, owned, owned, owned, flat, owned, owned,
                flat, P(None, ("gx", "gy")), flat, grid)
    return jax.shard_map(
        functools.partial(local, (n_gx, n_gy // n_z, n_z)), mesh=mesh, in_specs=in_specs,
        out_specs=(grid, owned, P()), check_vma=False)
```

profile of v0, /device:TPU:1, one launch (start us, length us, event | category | flops | bytes accessed | tf_op | source)
XLA Modules:
  0.0 177.3 jit_solution(14820004818825456400)
XLA Ops:
  0.6 172.4 %shard_map.175 = (f32[32,16,128]{2,1,0:T(8,128)}, f32[32,4096]{1,0:T(8,128)}, f32[1,1]{1,0:T(1,128)}) custom-call(f32[32,16,128]{2,1,0:T(8,128)} %rock_rhs.1, f32[32,4096]{1,0:T(8,128)} %frac_rhs.1, f32[32,16,128]{2,1,0:T(8,128)} %perm.1, f32[32,16,128]{2,1,0:T(8,128)} %storage.1, f32[32,16,128]{2,1,0:T(8,128)} %pressure.1, f32[32,4096]{1,0:T(8,128)} %frac_perm.1, ...), custom_call_target="tpu_custom_call" | custom-call | tf_op jit(solution)/shard_map/pallas_call | solution.py:570
  173.0 0.0 copy-start
  173.1 1.7 copy.22
  174.8 0.0 copy-done
  174.8 0.8 copy.23
Async XLA Ops:
  173.0 1.7 copy-start
where the time goes:
time: 177 us
  Pallas kernels  172 us (97%)
  local copies, waits for them, and re-layouts  2.52 us (1%)
  between operations  2.42 us (1%)
    pallas_call x1, Pallas kernels, local(): pl.pallas_call(functools.partial(kernel, sizes), out_shape=(jax.ShapeDtyp...  172 us

commit v1 on v0

--- a/solution.py
+++ b/solution.py
@@ -37,6 +37,12 @@
     return lax.dot_general(a, b, (((1,), (1,)), ((), ())), preferred_element_type=f32)
 
 
+def inverse(x):
+    guess = pl.reciprocal(x, approx=True)
+    guess = guess * (2.0 - x * guess)
+    return guess * (2.0 - x * guess)
+
+
 def lanes_of(table, index):
     return jnp.take_along_axis(table, index, axis=1)
 
@@ -46,10 +52,10 @@
     rock_rhs, frac_rhs, perm, storage, pressure, frac_perm, frac_storage, frac_pressure,
     geom, count, frac_cell, rock_cell, offset, pairs, cross_geom, agg,
     rock_out, frac_out, res_out,
-    Z0, E, PA, PE, WX, WYM, WYP, WZM, WZP, RD, INVR, W1R, Q, S, DEL, SEG,
+    Z0, E, PA, PE, WX, WYM, WYP, WZM, WZP, RD, INVR, W1R, Q, S, DEL,
     FD, INVF, TAP, TAM, TCP, TCM, W1F, ZF, F2, S2,
-    U, LV, BF, XU, LVX, XV, IDX, OFF, CPL, PICK, HV, AGS, VALS,
-    sx, rx, sy, ry, sic, ric, sag, rag, szy, rzy, sfl, rfl, sans, rans, scs, rcs,
+    U, LH, LV, TT, TF, BF, XU, LVX, AX, AY, AG, FI, XV, IDX, OFF, CPL, PICK, HV, AGS, VALS,
+    sx, rx, sy, ry, sic, ric, szy, rzy, sfl, rfl, sans, rans, scs, rcs,
     AR0, AR1, AR2, send_sem, recv_sem,
 ):
     n_gx, n_y, n_z = sizes
@@ -87,6 +93,7 @@
     lane16 = iota((16, 128), 1)
     lane32 = iota((32, 128), 1)
     row_lane = iota((1, 128), 1)
+    short_rows = iota((ROWS, 128), 0).astype(jnp.int16)
 
     def to_table(get):
         def body(r):
@@ -110,102 +117,127 @@
     def end_cells(e, h):
         return pairs[e : e + 1, h * 128 : (h + 1) * 128]
 
+    def turn(get, blocks, out, exact=False):
+        for m in range(blocks):
+            block = get(m).T
+            if exact:
+                out[0:128, m * 128 : (m + 1) * 128] = block.astype(bf16)
+            else:
+                high, low = halves(block)
+                out[0:128, m * 128 : (m + 1) * 128] = high
+                out[128:256, m * 128 : (m + 1) * 128] = low
+
     def pick_ends():
-        low = [jnp.broadcast_to(end_cells(e, h) & 127, (8, 128)) for e, h in ends]
-        high = [(end_cells(e, h) >> 7) - sub8 for e, h in ends]
-
-        def body(i, accs):
-            for j in range(4):
-                row = pl.multiple_of(i * 32 + j * 8, 8)
-                table = F2[pl.ds(row, 8), :]
-                accs = tuple(
-                    jnp.where(high[n] == row, lanes_of(table, low[n]), accs[n])
-                    for n in range(4)
-                )
-            return accs
-        accs = lax.fori_loop(0, FR * SLABS // 32, body, (jnp.zeros((8, 128), f32),) * 4)
-        return [jnp.sum(a, axis=0, keepdims=True) for a in accs]
-
-    def spread_frac(slot_vals, end_vals):
+        turn(lambda m: F2[m * 128 : (m + 1) * 128, :], 8, TF)
+        got = jnp.dot(TF[...], XU[...], preferred_element_type=f32)
+        got = got[0:128] + got[128:256]
+        return [
+            jnp.sum(jnp.where(sub128 == (end_cells(e, h) & 127),
+                              got[:, n * 128 : (n + 1) * 128], 0.0), axis=0, keepdims=True)
+            for n, (e, h) in enumerate(ends)
+        ]
+
+    def spread_ends(end_vals):
         for n, (e, h) in enumerate(ends):
             hot = sub128 == (end_cells(e, h) & 127)
-            high, low = halves(end_vals[n])
-            LVX[0:128, n * 128 : (n + 1) * 128] = jnp.where(hot, high.astype(f32), 0.0).astype(bf16)
-            LVX[128:256, n * 128 : (n + 1) * 128] = jnp.where(hot, low.astype(f32), 0.0).astype(bf16)
-        for m in range(4):
-            part = nt_dot(XU[m * 256 : (m + 1) * 256, :], LVX[...])
-            S2[m * 256 : (m + 1) * 256, :] = part[:, :128] + part[:, 128:]
-
+            high = end_vals[n].astype(bf16).astype(f32)
+            low = end_vals[n] - high
+            LVX[0:128, n * 128 : (n + 1) * 128] = jnp.where(hot, high, 0.0).astype(bf16)
+            LVX[128:256, n * 128 : (n + 1) * 128] = jnp.where(hot, low, 0.0).astype(bf16)
+        part = nt_dot(XU[...], LVX[...])
+        S2[...] = part[:, :128] + part[:, 128:]
+
+    def spread_slots(slot_vals):
         def body(f):
             cell = frac_cell[pl.ds(f, 1), :]
             high, low = halves(jnp.where(sub32 == cell >> 7, slot_vals[pl.ds(f, 1), :], 0.0))
             part = nt_dot(jnp.concatenate([high, low], axis=0), BF[f])
             rows = pl.ds(pl.multiple_of(f * SLABS, SLABS), SLABS)
             S2[rows, :] = S2[rows, :] + part[:32] + part[32:]
-        loop(FR, body, 2)
+        loop(FR, body, FR)
 
     def build_hot(src):
         def body(f):
-            high = IDX[src, pl.ds(f, 1), :] >> 7
-            for m in range(4):
-                hot = (sub128 + m * 128 == high).astype(f32).astype(bf16)
-                U[src, m * 128 : (m + 1) * 128, slab(f)] = hot
-        loop(FR, body)
+            cell = jnp.broadcast_to(IDX[src, pl.ds(f, 1), :], (16, 128))
+            high = jnp.concatenate([(cell >> 7).astype(jnp.int16)] * 32, axis=0)
+            low = jnp.concatenate([(cell & 127).astype(jnp.int16)] * 8, axis=0)
+            U[src, :, slab(f)] = jnp.where(short_rows == high, bf16(1), bf16(0))
+            LH[src, :, slab(f)] = jnp.where(short_rows[:128] == low, bf16(1), bf16(0))
+        loop(FR, body, 2)
 
     def spread_rock(src, vals, first):
         def body(f):
-            hot = sub128 == (IDX[src, pl.ds(f, 1), :] & 127)
-            high, low = halves(vals[pl.ds(f, 1), :])
-            LV[0:128, slab(f)] = jnp.where(hot, high.astype(f32), 0.0).astype(bf16)
-            LV[128:256, slab(f)] = jnp.where(hot, low.astype(f32), 0.0).astype(bf16)
-        loop(FR, body, 2)
-        for m in range(2):
-            part = nt_dot(U[src, m * 256 : (m + 1) * 256, :], LV[...])
-            total = part[:, :128] + part[:, 128:]
-            rows = pl.ds(m * 256, 256)
-            DEL[rows, :] = total if first else DEL[rows, :] + total
-
-    def pick_rock(get, outs):
-        def body(f):
-            cells = [IDX[src, pl.ds(f, 1), :] for src in range(3)]
-            low = [jnp.broadcast_to(c & 127, (8, 128)) for c in cells]
-            high = [(c >> 7) - sub8 for c in cells]
-            accs = [jnp.zeros((8, 128), f32)] * 3
-            for i in range(CX):
-                for j in range(2):
-                    table = get(i, j)
-                    row = i * 16 + j * 8
-                    accs = [
-                        jnp.where(high[n] == row, lanes_of(table, low[n]), accs[n])
-                        for n in range(3)
-                    ]
-            for n in range(3):
-                outs[n][pl.ds(f, 1), :] = jnp.sum(accs[n], axis=0, keepdims=True)
-        loop(FR, body)
+            value = vals[pl.ds(f, 1), :]
+            high = value.astype(bf16).astype(f32)
+            hot = LH[src, :, slab(f)]
+            for m, part in enumerate((high, value - high)):
+                part = jnp.broadcast_to(part, (16, 128)).astype(bf16)
+                LV[m * 128 : m * 128 + 128, slab(f)] = hot * jnp.concatenate([part] * 8, axis=0)
+        loop(FR, body, FR)
+        part = nt_dot(U[src], LV[...])
+        total = part[:, :128] + part[:, 128:]
+        DEL[...] = total if first else DEL[...] + total
+
+    def pick_rock(get, outs, agg_outs=None):
+        turn(get, 4, TT)
+        if agg_outs:
+            for m in range(4):
+                block = agg[m * 8 : m * 8 + 8].astype(f32).reshape(128, 128).T
+                TT[256:384, m * 128 : (m + 1) * 128] = block.astype(bf16)
+        table = TT[...] if agg_outs else TT[0:256]
+        for src in range(3):
+            got = jnp.dot(table, U[src], preferred_element_type=f32)
+            for f in range(FR):
+                row, here = slice(f, f + 1), slice(f * 128, f * 128 + 128)
+                hot = sub128 == IDX[src, row, :] & 127
+                value = got[0:128, here] + got[128:256, here]
+                outs[src][row, :] = jnp.sum(jnp.where(hot, value, 0.0), axis=0, keepdims=True)
+                if agg_outs:
+                    agg_outs[src][row, :] = jnp.sum(
+                        jnp.where(hot, got[256:384, here], 0.0), axis=0, keepdims=True)
+
+    def agg_cells(b, h):
+        cells = agg[2 * b + h]
+        return cells, pl.ds(pl.multiple_of(b * 256 + h * 128, 128), 128)
+
+    def build_aggregates():
+        def body(b):
+            for h in (0, 1):
+                cells, here = agg_cells(b, h)
+                cells = (cells & 15).astype(jnp.int16)
+                for a in range(16):
+                    AY[a * 16 : a * 16 + 16, here] = jnp.where(
+                        cells == jnp.int16(a), bf16(1), bf16(0))
+        loop(16, body, 2)
+        place = iota((256, 128), 0) >> 4 == iota((256, 128), 1) & 15
+        AG[...] = place.astype(f32).astype(bf16)
 
     def aggregate_sums(src):
-        for chunk in range(4):
-            def body(i, accs):
-                for j in (0, 8):
-                    value, number = src[i, j : j + 8, :], agg[i, j : j + 8, :]
-                    accs = tuple(
-                        acc + jnp.where(number == chunk * 16 + a, value, 0.0)
-                        for a, acc in enumerate(accs)
-                    )
-                return accs
-            accs = lax.fori_loop(0, CX, body, (jnp.zeros((8, 128), f32),) * 16)
-            for a, acc in enumerate(accs):
-                SEG[chunk * 16 + a : chunk * 16 + a + 1, :] = jnp.sum(acc, axis=0, keepdims=True)
-        ones = jnp.ones((16, 128), bf16)
-        rest = SEG[...]
-        total = jnp.zeros((16, 128), f32)
+        def body(b):
+            for h in (0, 1):
+                cells, here = agg_cells(b, h)
+                cells = cells >> 4
+                value = src[2 * b + h]
+                high = value.astype(bf16).astype(f32)
+                low = value - high
+                for a in range(4):
+                    AX[a * 32 : a * 32 + 16, here] = jnp.where(cells == a, high, 0.0).astype(bf16)
+                    AX[a * 32 + 16 : a * 32 + 32, here] = jnp.where(cells == a, low, 0.0).astype(bf16)
+        loop(16, body, 8)
+        part = nt_dot(AX[...], AY[...])
+        part = jnp.where(iota((128, 256), 0) & 15 == iota((128, 256), 1) & 15, part, 0.0)
+        rest = jnp.concatenate([fold(part[a * 32 : a * 32 + 32]) for a in range(4)], axis=0)
+        pieces = []
         for _ in range(3):
-            high = rest.astype(bf16)
-            rest = rest - high.astype(f32)
-            total = total + nt_dot(ones, high)
-        return total
-
-    SEG[NAGG:128, :] = jnp.zeros((128 - NAGG, 128), f32)
+            pieces.append(rest.astype(bf16))
+            rest = rest - pieces[-1].astype(f32)
+        total = jnp.dot(jnp.concatenate(pieces, axis=0), AG[...], preferred_element_type=f32)
+        total = total[0:32] + total[32:64] + total[64:96]
+        total = jnp.where(sub32 >> 3 == lane32 >> 4, total, 0.0)
+        return jnp.broadcast_to(jnp.sum(total, axis=0, keepdims=True), (16, 128))
+
+    def fold(x):
+        return sum(x[j : j + 8] for j in range(0, x.shape[0], 8))
 
     to_table(lambda r: frac_pressure[:, slab(r)])
     pick_slots(PICK)
@@ -221,7 +253,7 @@
         sic[1, 0, row, :] = jnp.where(live & (where == -1), cell, -1).astype(f32)
         value = jnp.where(live, geom[row, :] * jnp.exp(-0.5 * PICK[row, :]), 0.0)
         CPL[row, :] = value
-    loop(FR, split_slots, 2)
+    loop(FR, split_slots, 4)
     sic[0, 1] = CPL[...]
     sic[1, 1] = CPL[...]
 
@@ -239,39 +271,41 @@
     faces_sent = [send(sx.at[d], rx.at[d], x_dev[d]) for d in (0, 1)]
     faces_sent += [send(sy.at[d], ry.at[d], y_dev[d]) for d in (0, 1)]
 
+    def scale_frac(r):
+        press = frac_pressure[:, slab(r)]
+        TCM[:, slab(r)] = frac_perm[:, slab(r)] * jnp.exp(-0.25 * press)
+    loop(SLABS, scale_frac, 4)
+
     def face_along(r):
-        conduct, press = frac_perm[:, slab(r)], frac_pressure[:, slab(r)]
-        scaled = conduct * jnp.exp(-0.25 * press)
-        F2[pl.ds(r, FR, stride=SLABS), :] = press
+        conduct, scaled = frac_perm[:, slab(r)], TCM[:, slab(r)]
         near, near_scaled = pltpu.roll(conduct, 127, 1), pltpu.roll(scaled, 127, 1)
-        weight = 2.0 * scaled * near_scaled / (conduct + near)
-        weight = jnp.where(lane32 % FSIDE < FSIDE - 1, weight, 0.0)
+        weight = 2.0 * scaled * near_scaled * inverse(conduct + near)
+        weight = jnp.where(lane32 & (FSIDE - 1) < FSIDE - 1, weight, 0.0)
         TAP[:, slab(r)] = weight
         TAM[:, slab(r)] = pltpu.roll(weight, 1, 1)
         after = slab(jnp.minimum(r + 1, SLABS - 1))
-        next_conduct = frac_perm[:, after]
-        next_scaled = next_conduct * jnp.exp(-0.25 * frac_pressure[:, after])
         first = lane32 < FSIDE
-        near = pltpu.roll(jnp.where(first, next_conduct, conduct), FSIDE, 1)
-        near_scaled = pltpu.roll(jnp.where(first, next_scaled, scaled), FSIDE, 1)
-        weight = 2.0 * scaled * near_scaled / (conduct + near)
+        near = pltpu.roll(jnp.where(first, frac_perm[:, after], conduct), FSIDE, 1)
+        near_scaled = pltpu.roll(jnp.where(first, TCM[:, after], scaled), FSIDE, 1)
+        weight = 2.0 * scaled * near_scaled * inverse(conduct + near)
         TCP[:, slab(r)] = jnp.where(first | (r < SLABS - 1), weight, 0.0)
-    loop(SLABS, face_along)
-
-    pressures = pick_ends()
+    loop(SLABS, face_along, 4)
+
     for n, (e, h) in enumerate(ends):
         for m in range(8):
             hot = (sub128 + m * 128 == end_cells(e, h) >> 7).astype(f32).astype(bf16)
             XU[m * 128 : (m + 1) * 128, n * 128 : (n + 1) * 128] = hot
+    pressures = pick_ends()
     for h in (0, 1):
         XV[h : h + 1, :] = cross_geom[0:1, h * 128 : (h + 1) * 128] * jnp.exp(
             -0.25 * (pressures[h] + pressures[h + 2]))
 
     def build_lanes(f):
         BF[f] = (sub128 == (frac_cell[pl.ds(f, 1), :] & 127)).astype(f32).astype(bf16)
-    loop(FR, build_lanes)
+    loop(FR, build_lanes, 2)
     coefs = [XV[h : h + 1, :] for h in (0, 1)]
-    spread_frac(CPL, coefs + coefs)
+    spread_ends(coefs + coefs)
+    spread_slots(CPL)
 
     def face_back(r):
         before = slab(jnp.maximum(r - 1, 0))
@@ -283,15 +317,15 @@
         diag = frac_storage[:, slab(r)] + TAP[:, slab(r)] + TAM[:, slab(r)] + own + back
         diag = diag + S2[pl.ds(r, FR, stride=SLABS), :]
         FD[:, slab(r)] = diag
-        INVF[:, slab(r)] = relaxation / diag
-    loop(SLABS, face_back)
+        INVF[:, slab(r)] = relaxation * inverse(diag)
+    loop(SLABS, face_back, 4)
 
     def smooth_frac(k, source):
         def body(r):
             z = source[:, slab(r)] * INVF[:, slab(r)]
             ZF[k, :, slab(r)] = z
             F2[pl.ds(r, FR, stride=SLABS), :] = z
-        loop(SLABS, body, 2)
+        loop(SLABS, body, 4)
         pick_slots(PICK)
         sfl[k] = CPL[...] * PICK[...]
         return [send(sfl.at[k], rfl.at[k, d], y_dev[d]) for d in (0, 1)]
@@ -306,9 +340,7 @@
         IDX[1 + d] = ric[d, 0].astype(jnp.int32)
         build_hot(1 + d)
         spread_rock(1 + d, ric.at[d, 1], False)
-    pick_rock(lambda i, j: agg[i, j * 8 : j * 8 + 8, :].astype(f32), [AGS, sag.at[0], sag.at[1]])
-    aggs_sent = [send(sag.at[1 - d], rag.at[d], y_dev[d]) for d in (0, 1)]
-
+    build_aggregates()
     for copy in faces_sent:
         copy.wait_recv()
     open_x = [gx > 0, gx < n_gx - 1]
@@ -318,7 +350,7 @@
         conduct = perm[i]
         PA[i + 1] = conduct
         PE[i + 1] = conduct * jnp.exp(-0.25 * pressure[i])
-    loop(CX, scale_rock)
+    loop(CX, scale_rock, 4)
     for d, plane in enumerate((0, CX + 1)):
         conduct = jnp.where(open_x[d], rx[d, 0], 0.0)
         PA[plane] = conduct
@@ -334,28 +366,32 @@
     def above(x, edge):
         return jnp.where(sub16 == CY - 1, edge, pltpu.roll(x, CY - 1, 0))
 
+    def face(conduct, scaled, near, near_scaled):
+        return 2.0 * scaled * near_scaled * inverse(conduct + near)
+
+    VALS[0] = face(perm[:, 0, :], PE[1 : CX + 1, 0, :], ry[0, 0], ry[0, 1])
+
     def rock_faces(i):
         conduct, scaled = PA[i + 1], PE[i + 1]
         row = pl.ds(i, 1)
-
-        def weight(near, near_scaled):
-            return 2.0 * scaled * near_scaled / (conduct + near)
-        WX[i] = weight(PA[i], PE[i])
-        WYM[i] = weight(below(conduct, ry[0, 0, row, :]), below(scaled, ry[0, 1, row, :]))
-        WYP[i] = weight(above(conduct, ry[1, 0, row, :]), above(scaled, ry[1, 1, row, :]))
-        up = weight(pltpu.roll(conduct, 127, 1), pltpu.roll(scaled, 127, 1))
+        WX[i] = face(conduct, scaled, PA[i], PE[i])
+        side = face(conduct, scaled, above(conduct, ry[1, 0, row, :]),
+                    above(scaled, ry[1, 1, row, :]))
+        WYP[i] = side
+        WYM[i] = below(side, VALS[0, row, :])
+        up = face(conduct, scaled, pltpu.roll(conduct, 127, 1), pltpu.roll(scaled, 127, 1))
         up = jnp.where(lane16 < NZ - 1, up, 0.0)
         WZP[i] = up
         WZM[i] = pltpu.roll(up, 1, 1)
-    loop(CX, rock_faces)
-    WX[CX] = 2.0 * PE[CX] * PE[CX + 1] / (PA[CX] + PA[CX + 1])
+    loop(CX, rock_faces, 4)
+    WX[CX] = face(PA[CX], PE[CX], PA[CX + 1], PE[CX + 1])
 
     def rock_diagonal(i):
         faces = [WX[i], WX[i + 1], WYM[i], WYP[i], WZM[i], WZP[i]]
         rows = pl.ds(pl.multiple_of(i * CY, CY), CY)
         diag = storage[i] + sum(faces) + DEL[rows, :]
         RD[i] = diag
-        INVR[i] = relaxation / diag
+        INVR[i] = relaxation * inverse(diag)
         mine = agg[i]
         inside = lambda n: jnp.clip(n, 0, CX - 1)
         nears = [
@@ -367,9 +403,9 @@
         for face, near in zip(faces, nears):
             diag = diag - jnp.where(near == mine, face, 0.0)
         S[i] = diag
-    loop(CX, rock_diagonal)
+    loop(CX, rock_diagonal, 4)
     coarse_diag = aggregate_sums(S)
-    coarse_diag = jnp.where(lane16 < NAGG, coarse_diag, 1.0)
+    inverse_coarse = 1.0 / jnp.where(lane16 < NAGG, coarse_diag, 1.0)
 
     def stencil(i, center, low_x, high_x, low_y, high_y):
         out = RD[i] * center
@@ -377,20 +413,21 @@
         out = out - WYM[i] * below(center, low_y) - WYP[i] * above(center, high_y)
         return out - WZM[i] * pltpu.roll(center, 1, 1) - WZP[i] * pltpu.roll(center, 127, 1)
 
-    def iterate(k, rock_vec, frac_vec, flux_sent):
-        def smooth_rock(i):
-            Z0[k, i + 1] = rock_vec[i] * INVR[i]
-        loop(CX, smooth_rock, 2)
+    def send_faces(k):
         for d, row in enumerate((CY - 1, 0)):
             szy[k, d] = Z0[k, 1 : CX + 1, row, :]
-        halo_sent = [
+        return [
             send(Z0.at[k, CX], Z0.at[k, 0], x_dev[0]),
             send(Z0.at[k, 1], Z0.at[k, CX + 1], x_dev[1]),
         ] + [send(szy.at[k, d], rzy.at[k, d], y_dev[d]) for d in (0, 1)]
-        pick_rock(lambda i, j: Z0[k, i + 1, j * 8 : j * 8 + 8, :],
-                  [HV, sans.at[k, 0], sans.at[k, 1]])
-        answers_sent = [send(sans.at[k, 1 - d], rans.at[k, d], y_dev[d]) for d in (0, 1)]
-        values = pick_ends()
+
+    def iterate(k, rock_vec, frac_vec, halo_sent, flux_sent):
+        pick_rock(lambda m: Z0[k, m * 8 + 1 : m * 8 + 9].reshape(128, 128),
+                  [HV, sans.at[k, 0, 0], sans.at[k, 1, 0]],
+                  None if k else [AGS, sans.at[k, 0, 1], sans.at[k, 1, 1]])
+        parts = 1 if k else 2
+        answers_sent = [
+            send(sans.at[k, 1 - d, 0:parts], rans.at[k, d, 0:parts], y_dev[d]) for d in (0, 1)]
         spread_rock(0, sfl.at[k], True)
         for d, copy in enumerate(flux_sent):
             copy.wait_recv()
@@ -405,21 +442,37 @@
                             rzy[k, 0, row, :], rzy[k, 1, row, :]) - DEL[rows, :]
             Q[i] = image
             S[i] = rock_vec[i] - image
-        loop(CX, residual)
-        coarse = aggregate_sums(S) / coarse_diag
+        loop(CX, residual, 8)
+        coarse = aggregate_sums(S) * inverse_coarse
         scs[k] = coarse[0:8]
         coarse_sent = [send(scs.at[k], rcs.at[k, d], x_dev[d]) for d in (0, 1)]
         coarse_sent += [send(scs.at[k], rcs.at[k, 2 + d], y_dev[d]) for d in (0, 1)]
 
+        values = pick_ends()
+        coefs = [XV[h : h + 1, :] for h in (0, 1)]
+        spread_ends([coefs[h] * values[2 * (1 - e) + h] for e, h in ends])
+
         def correct(i):
             E[k, i + 1] = lanes_of(coarse, agg[i])
-        loop(CX, correct, 2)
-        if k == 0:
-            for copy in aggs_sent:
-                copy.wait_recv()
-            AGS[...] = AGS[...] + rag[0] + rag[1]
+        loop(CX, correct, 8)
+
+        def frac_faces(r):
+            here = slab(r)
+            z = ZF[k, :, here]
+            before = ZF[k, :, slab(jnp.maximum(r - 1, 0))]
+            after = ZF[k, :, slab(jnp.minimum(r + 1, SLABS - 1))]
+            first = lane32 < FSIDE
+            down = pltpu.roll(jnp.where(first, after, z), FSIDE, 1)
+            up = pltpu.roll(jnp.where(first, z, before), FSIDE, 1)
+            image = FD[:, here] * z
+            image = image - TAP[:, here] * pltpu.roll(z, 127, 1) - TAM[:, here] * pltpu.roll(z, 1, 1)
+            image = image - TCP[:, here] * down - TCM[:, here] * up
+            FI[:, here] = image - relaxation * frac_vec[:, here]
+        loop(SLABS, frac_faces, 4)
         for copy in answers_sent + coarse_sent:
             copy.wait_recv()
+        if k == 0:
+            AGS[...] = AGS[...] + rans[0, 0, 1] + rans[0, 1, 1]
         tables = [jnp.concatenate([rcs[k, d], rcs[k, d]], axis=0) for d in range(4)]
         for d, plane in enumerate((0, CX + 1)):
             E[k, plane] = lanes_of(tables[d], rx[d, 2].astype(jnp.int32))
@@ -430,16 +483,11 @@
         four = [jnp.concatenate([t] * 2, axis=0) for t in (coarse, tables[2], tables[3])]
         own, low, high = [lanes_of(t, slot_agg) for t in four]
         where = OFF[...]
-        host = HV[...] + rans[k, 0] + rans[k, 1]
+        host = HV[...] + rans[k, 0, 0] + rans[k, 1, 0]
         host = host + jnp.where(where == 0, own, jnp.where(where < 0, low, high))
         VALS[2] = CPL[...] * host
-        coefs = [XV[h : h + 1, :] for h in (0, 1)]
-        spread_frac(VALS.at[2], [coefs[h] * values[2 * (1 - e) + h] for e, h in ends])
 
         zero = jnp.zeros((8, 128), f32)
-
-        def fold(x):
-            return sum(x[j : j + 8] for j in range(0, x.shape[0], 8))
 
         def products(x, v, b):
             if k == 0:
@@ -454,30 +502,28 @@
             image = image - relaxation * vec
             if k == 0:
                 W1R[i] = image
+                Z0[1, i + 1] = image * INVR[i]
             return tuple(a + p for a, p in zip(accs, products(image, vec, rock_rhs[i])))
-        accs = lax.fori_loop(0, CX, rock_image, (zero,) * 3)
+        accs = lax.fori_loop(0, CX, rock_image, (zero,) * 3, unroll=8)
+        halo_sent = send_faces(1) if k == 0 else None
+        spread_slots(VALS.at[2])
 
         def frac_image(r, accs):
             here = slab(r)
             vec = frac_vec[:, here]
-            z = ZF[k, :, here]
-            before = ZF[k, :, slab(jnp.maximum(r - 1, 0))]
-            after = ZF[k, :, slab(jnp.minimum(r + 1, SLABS - 1))]
-            first = lane32 < FSIDE
-            down = pltpu.roll(jnp.where(first, after, z), FSIDE, 1)
-            up = pltpu.roll(jnp.where(first, z, before), FSIDE, 1)
-            image = FD[:, here] * z - S2[pl.ds(r, FR, stride=SLABS), :]
-            image = image - TAP[:, here] * pltpu.roll(z, 127, 1) - TAM[:, here] * pltpu.roll(z, 1, 1)
-            image = image - TCP[:, here] * down - TCM[:, here] * up
-            image = image - relaxation * vec
+            image = FI[:, here] - S2[pl.ds(r, FR, stride=SLABS), :]
             if k == 0:
                 W1F[:, here] = image
             return tuple(a + p for a, p in zip(accs, products(image, vec, frac_rhs[:, here])))
-        return lax.fori_loop(0, SLABS, frac_image, accs)
-
-    dots = list(iterate(0, rock_rhs, frac_rhs, flux_sent))
+        accs = lax.fori_loop(0, SLABS, frac_image, accs, unroll=4)
+        return list(accs), halo_sent
+
+    def smooth_rock(i):
+        Z0[0, i + 1] = rock_rhs[i] * INVR[i]
+    loop(CX, smooth_rock, 8)
+    dots, halo_sent = iterate(0, rock_rhs, frac_rhs, send_faces(0), flux_sent)
     flux_sent = smooth_frac(1, W1F)
-    dots += list(iterate(1, W1R, W1F, flux_sent))
+    dots += iterate(1, W1R, W1F, halo_sent, flux_sent)[0]
 
     tile = jnp.zeros((8, 128), f32)
     for n, part in enumerate(dots):
@@ -526,11 +572,11 @@
 
     def rock_update(i):
         rock_out[i] = on_b * (Z0[0, i + 1] + E[0, i + 1]) + on_p * (Z0[1, i + 1] + E[1, i + 1])
-    loop(CX, rock_update, 2)
+    loop(CX, rock_update, 8)
 
     def frac_update(r):
         frac_out[:, slab(r)] = on_b * ZF[0, :, slab(r)] + on_p * ZF[1, :, slab(r)]
-    loop(SLABS, frac_update, 2)
+    loop(SLABS, frac_update, 8)
     for copy in started:
         copy.wait_send()
 
@@ -553,17 +599,19 @@
 
     scratch = [
         mem(2, *tall), mem(2, *tall), mem(*tall), mem(*tall), mem(CX + 1, CY, NZ),
-        *[mem(*block) for _ in range(9)], mem(ROWS, 128), mem(128, 128),
+        *[mem(*block) for _ in range(9)], mem(ROWS, 128),
         *[mem(*frac) for _ in range(7)], mem(2, *frac), mem(FR * SLABS, 128), mem(FR * SLABS, 128),
-        mem(3, ROWS, FR * KC, kind=bf16), mem(256, FR * KC, kind=bf16),
+        mem(3, ROWS, FR * KC, kind=bf16), mem(3, 128, FR * KC, kind=bf16),
+        mem(256, FR * KC, kind=bf16), mem(384, ROWS, kind=bf16), mem(256, FR * SLABS, kind=bf16),
         mem(FR, 128, 128, kind=bf16), mem(FR * SLABS, 2 * CROSS, kind=bf16),
-        mem(256, 2 * CROSS, kind=bf16), mem(8, 128),
+        mem(256, 2 * CROSS, kind=bf16), mem(128, 4096, kind=bf16), mem(256, 4096, kind=bf16),
+        mem(256, 128, kind=bf16), mem(*frac), mem(8, 128),
         mem(3, *slot, kind=jnp.int32), mem(*slot, kind=jnp.int32),
         mem(*slot), mem(*slot), mem(*slot), mem(*slot), mem(3, *slot),
         mem(2, 3, CY, NZ), mem(2, 3, CY, NZ), mem(2, 3, CX, NZ), mem(2, 3, CX, NZ),
-        mem(2, 2, *slot), mem(2, 2, *slot), mem(2, *slot), mem(2, *slot),
+        mem(2, 2, *slot), mem(2, 2, *slot),
         mem(2, 2, CX, NZ), mem(2, 2, CX, NZ), mem(2, *slot), mem(2, 2, *slot),
-        mem(2, 2, *slot), mem(2, 2, *slot), mem(2, 8, 128), mem(2, 4, 8, 128),
+        mem(2, 2, 2, *slot), mem(2, 2, 2, *slot), mem(2, 8, 128), mem(2, 4, 8, 128),
         mem(n_gx, 8, 128), mem(n_y, 8, 128), mem(n_z, 8, 128),
         pltpu.SemaphoreType.DMA((64,)), pltpu.SemaphoreType.DMA((64,)),
     ]

time: 177 us -> 93.9 us (0.53)
  Pallas kernels: 172 us -> 88.9 us
    pallas_call x1, Pallas kernels: 172 us -> 88.9 us  [local(): pl.pallas_call(functools.partial(kernel, sizes), out_shape=(jax.ShapeDtyp...]
where the time goes in v1:
time: 93.9 us; the launch traced here: 93.8 us
  Pallas kernels  88.9 us (95%)
  local copies, waits for them, and re-layouts  2.52 us (3%)
  between operations  2.42 us (3%)
    pallas_call x1, Pallas kernels, local(): pl.pallas_call(functools.partial(kernel, sizes), out_shape=(jax.ShapeDtyp...  88.9 us
    unnamed x4, local copies, waits for them, and re-layouts  2.52 us

profile of v1, /device:TPU:1, one launch (start us, length us, event | category | flops | bytes accessed | tf_op | source)
XLA Modules:
  0.0 93.8 jit_solution(1183404677934067861)
XLA Ops:
  0.6 88.9 %shard_map.175 = (f32[32,16,128]{2,1,0:T(8,128)}, f32[32,4096]{1,0:T(8,128)}, f32[1,1]{1,0:T(1,128)}) custom-call(f32[32,16,128]{2,1,0:T(8,128)} %rock_rhs.1, f32[32,4096]{1,0:T(8,128)} %frac_rhs.1, f32[32,16,128]{2,1,0:T(8,128)} %perm.1, f32[32,16,128]{2,1,0:T(8,128)} %storage.1, f32[32,16,128]{2,1,0:T(8,128)} %pressure.1, f32[32,4096]{1,0:T(8,128)} %frac_perm.1, ...), custom_call_target="tpu_custom_call" | custom-call | tf_op jit(solution)/shard_map/pallas_call | solution.py:618
  89.5 0.0 copy-start
  89.5 1.7 %copy.22 = f32[32,16,128]{2,1,0:T(8,128)} copy(f32[32,16,128]{2,1,0:T(8,128)} %get-tuple-element.12) | data formatting | bytes 524288
  91.2 0.0 copy-done
  91.2 0.8 copy.23
Async XLA Ops:
  89.5 1.7 %copy-start = (f32[32,4096]{1,0:T(8,128)S(1)}, f32[32,4096]{1,0:T(8,128)}, u32[]{:S(2)}) copy-start(f32[32,4096]{1,0:T(8,128)} %get-tuple-element.13) | copy-start | bytes 1572868

commit v2 on v1

--- a/solution.py
+++ b/solution.py
@@ -16,36 +16,30 @@
 relaxation = 0.8
 epsilon = 1e-06
 MESH = pl.DeviceIdType.MESH
+UB, UF, UR = 32, 32, 32
 f32 = jnp.float32
 bf16 = jnp.bfloat16
 
-
 def iota(shape, dim):
     return lax.broadcasted_iota(jnp.int32, shape, dim)
 
-
 def loop(count, body, unroll=1):
     lax.fori_loop(0, count, lambda i, c: (body(i), c)[1], 0, unroll=unroll)
-
 
 def halves(x):
     high = x.astype(bf16)
     return high, (x - high.astype(f32)).astype(bf16)
 
-
 def nt_dot(a, b):
     return lax.dot_general(a, b, (((1,), (1,)), ((), ())), preferred_element_type=f32)
-
 
 def inverse(x):
     guess = pl.reciprocal(x, approx=True)
     guess = guess * (2.0 - x * guess)
     return guess * (2.0 - x * guess)
 
-
 def lanes_of(table, index):
     return jnp.take_along_axis(table, index, axis=1)
-
 
 def kernel(
     sizes,
@@ -54,7 +48,7 @@
     rock_out, frac_out, res_out,
     Z0, E, PA, PE, WX, WYM, WYP, WZM, WZP, RD, INVR, W1R, Q, S, DEL,
     FD, INVF, TAP, TAM, TCP, TCM, W1F, ZF, F2, S2,
-    U, LH, LV, TT, TF, BF, XU, LVX, AX, AY, AG, FI, XV, IDX, OFF, CPL, PICK, HV, AGS, VALS,
+    U, LV, TT, TF, BF, XU, LVX, AX, AY, AG, FI, XV, IDX, OFF, CPL, PICK, HV, AGS, VALS,
     sx, rx, sy, ry, sic, ric, szy, rzy, sfl, rfl, sans, rans, scs, rcs,
     AR0, AR1, AR2, send_sem, recv_sem,
 ):
@@ -110,7 +104,7 @@
             got = lanes_of(table, jnp.broadcast_to(cell & 127, (SLABS, 128)))
             out[pl.ds(f, 1), :] = jnp.sum(
                 jnp.where(sub32 == cell >> 7, got, 0.0), axis=0, keepdims=True)
-        loop(FR, body, 4)
+        loop(FR, body, 32)
 
     ends = [(e, h) for e in (0, 1) for h in (0, 1)]
 
@@ -160,19 +154,19 @@
         def body(f):
             cell = jnp.broadcast_to(IDX[src, pl.ds(f, 1), :], (16, 128))
             high = jnp.concatenate([(cell >> 7).astype(jnp.int16)] * 32, axis=0)
-            low = jnp.concatenate([(cell & 127).astype(jnp.int16)] * 8, axis=0)
             U[src, :, slab(f)] = jnp.where(short_rows == high, bf16(1), bf16(0))
-            LH[src, :, slab(f)] = jnp.where(short_rows[:128] == low, bf16(1), bf16(0))
-        loop(FR, body, 2)
+        loop(FR, body, UB)
 
     def spread_rock(src, vals, first):
         def body(f):
             value = vals[pl.ds(f, 1), :]
             high = value.astype(bf16).astype(f32)
-            hot = LH[src, :, slab(f)]
+            cell = jnp.broadcast_to(IDX[src, pl.ds(f, 1), :] & 127, (16, 128))
+            hot = short_rows[:128] == jnp.concatenate([cell.astype(jnp.int16)] * 8, axis=0)
             for m, part in enumerate((high, value - high)):
                 part = jnp.broadcast_to(part, (16, 128)).astype(bf16)
-                LV[m * 128 : m * 128 + 128, slab(f)] = hot * jnp.concatenate([part] * 8, axis=0)
+                part = jnp.concatenate([part] * 8, axis=0)
+                LV[m * 128 : m * 128 + 128, slab(f)] = jnp.where(hot, part, bf16(0))
         loop(FR, body, FR)
         part = nt_dot(U[src], LV[...])
         total = part[:, :128] + part[:, 128:]
@@ -223,7 +217,7 @@
                 for a in range(4):
                     AX[a * 32 : a * 32 + 16, here] = jnp.where(cells == a, high, 0.0).astype(bf16)
                     AX[a * 32 + 16 : a * 32 + 32, here] = jnp.where(cells == a, low, 0.0).astype(bf16)
-        loop(16, body, 8)
+        loop(16, body, 16)
         part = nt_dot(AX[...], AY[...])
         part = jnp.where(iota((128, 256), 0) & 15 == iota((128, 256), 1) & 15, part, 0.0)
         rest = jnp.concatenate([fold(part[a * 32 : a * 32 + 32]) for a in range(4)], axis=0)
@@ -274,7 +268,7 @@
     def scale_frac(r):
         press = frac_pressure[:, slab(r)]
         TCM[:, slab(r)] = frac_perm[:, slab(r)] * jnp.exp(-0.25 * press)
-    loop(SLABS, scale_frac, 4)
+    loop(SLABS, scale_frac, UF)
 
     def face_along(r):
         conduct, scaled = frac_perm[:, slab(r)], TCM[:, slab(r)]
@@ -289,7 +283,7 @@
         near_scaled = pltpu.roll(jnp.where(first, TCM[:, after], scaled), FSIDE, 1)
         weight = 2.0 * scaled * near_scaled * inverse(conduct + near)
         TCP[:, slab(r)] = jnp.where(first | (r < SLABS - 1), weight, 0.0)
-    loop(SLABS, face_along, 4)
+    loop(SLABS, face_along, UF)
 
     for n, (e, h) in enumerate(ends):
         for m in range(8):
@@ -303,6 +297,7 @@
     def build_lanes(f):
         BF[f] = (sub128 == (frac_cell[pl.ds(f, 1), :] & 127)).astype(f32).astype(bf16)
     loop(FR, build_lanes, 2)
+
     coefs = [XV[h : h + 1, :] for h in (0, 1)]
     spread_ends(coefs + coefs)
     spread_slots(CPL)
@@ -318,14 +313,14 @@
         diag = diag + S2[pl.ds(r, FR, stride=SLABS), :]
         FD[:, slab(r)] = diag
         INVF[:, slab(r)] = relaxation * inverse(diag)
-    loop(SLABS, face_back, 4)
+    loop(SLABS, face_back, UF)
 
     def smooth_frac(k, source):
         def body(r):
             z = source[:, slab(r)] * INVF[:, slab(r)]
             ZF[k, :, slab(r)] = z
             F2[pl.ds(r, FR, stride=SLABS), :] = z
-        loop(SLABS, body, 4)
+        loop(SLABS, body, UF)
         pick_slots(PICK)
         sfl[k] = CPL[...] * PICK[...]
         return [send(sfl.at[k], rfl.at[k, d], y_dev[d]) for d in (0, 1)]
@@ -333,14 +328,18 @@
     flux_sent = smooth_frac(0, frac_rhs)
 
     build_hot(0)
+
     spread_rock(0, CPL, True)
+
     for copy in slots_sent:
         copy.wait_recv()
     for d in (0, 1):
         IDX[1 + d] = ric[d, 0].astype(jnp.int32)
         build_hot(1 + d)
         spread_rock(1 + d, ric.at[d, 1], False)
+
     build_aggregates()
+
     for copy in faces_sent:
         copy.wait_recv()
     open_x = [gx > 0, gx < n_gx - 1]
@@ -350,7 +349,7 @@
         conduct = perm[i]
         PA[i + 1] = conduct
         PE[i + 1] = conduct * jnp.exp(-0.25 * pressure[i])
-    loop(CX, scale_rock, 4)
+    loop(CX, scale_rock, UR)
     for d, plane in enumerate((0, CX + 1)):
         conduct = jnp.where(open_x[d], rx[d, 0], 0.0)
         PA[plane] = conduct
@@ -383,7 +382,7 @@
         up = jnp.where(lane16 < NZ - 1, up, 0.0)
         WZP[i] = up
         WZM[i] = pltpu.roll(up, 1, 1)
-    loop(CX, rock_faces, 4)
+    loop(CX, rock_faces, UR)
     WX[CX] = face(PA[CX], PE[CX], PA[CX + 1], PE[CX + 1])
 
     def rock_diagonal(i):
@@ -403,7 +402,8 @@
         for face, near in zip(faces, nears):
             diag = diag - jnp.where(near == mine, face, 0.0)
         S[i] = diag
-    loop(CX, rock_diagonal, 4)
+    loop(CX, rock_diagonal, UR)
+
     coarse_diag = aggregate_sums(S)
     inverse_coarse = 1.0 / jnp.where(lane16 < NAGG, coarse_diag, 1.0)
 
@@ -422,12 +422,14 @@
         ] + [send(szy.at[k, d], rzy.at[k, d], y_dev[d]) for d in (0, 1)]
 
     def iterate(k, rock_vec, frac_vec, halo_sent, flux_sent):
+
         pick_rock(lambda m: Z0[k, m * 8 + 1 : m * 8 + 9].reshape(128, 128),
                   [HV, sans.at[k, 0, 0], sans.at[k, 1, 0]],
                   None if k else [AGS, sans.at[k, 0, 1], sans.at[k, 1, 1]])
         parts = 1 if k else 2
         answers_sent = [
             send(sans.at[k, 1 - d, 0:parts], rans.at[k, d, 0:parts], y_dev[d]) for d in (0, 1)]
+
         spread_rock(0, sfl.at[k], True)
         for d, copy in enumerate(flux_sent):
             copy.wait_recv()
@@ -442,7 +444,8 @@
                             rzy[k, 0, row, :], rzy[k, 1, row, :]) - DEL[rows, :]
             Q[i] = image
             S[i] = rock_vec[i] - image
-        loop(CX, residual, 8)
+        loop(CX, residual, UR)
+
         coarse = aggregate_sums(S) * inverse_coarse
         scs[k] = coarse[0:8]
         coarse_sent = [send(scs.at[k], rcs.at[k, d], x_dev[d]) for d in (0, 1)]
@@ -454,7 +457,7 @@
 
         def correct(i):
             E[k, i + 1] = lanes_of(coarse, agg[i])
-        loop(CX, correct, 8)
+        loop(CX, correct, UR)
 
         def frac_faces(r):
             here = slab(r)
@@ -468,7 +471,8 @@
             image = image - TAP[:, here] * pltpu.roll(z, 127, 1) - TAM[:, here] * pltpu.roll(z, 1, 1)
             image = image - TCP[:, here] * down - TCM[:, here] * up
             FI[:, here] = image - relaxation * frac_vec[:, here]
-        loop(SLABS, frac_faces, 4)
+        loop(SLABS, frac_faces, UF)
+
         for copy in answers_sent + coarse_sent:
             copy.wait_recv()
         if k == 0:
@@ -504,8 +508,9 @@
                 W1R[i] = image
                 Z0[1, i + 1] = image * INVR[i]
             return tuple(a + p for a, p in zip(accs, products(image, vec, rock_rhs[i])))
-        accs = lax.fori_loop(0, CX, rock_image, (zero,) * 3, unroll=8)
+        accs = lax.fori_loop(0, CX, rock_image, (zero,) * 3, unroll=UR)
         halo_sent = send_faces(1) if k == 0 else None
+
         spread_slots(VALS.at[2])
 
         def frac_image(r, accs):
@@ -515,13 +520,14 @@
             if k == 0:
                 W1F[:, here] = image
             return tuple(a + p for a, p in zip(accs, products(image, vec, frac_rhs[:, here])))
-        accs = lax.fori_loop(0, SLABS, frac_image, accs, unroll=4)
+        accs = lax.fori_loop(0, SLABS, frac_image, accs, unroll=UF)
         return list(accs), halo_sent
 
     def smooth_rock(i):
         Z0[0, i + 1] = rock_rhs[i] * INVR[i]
-    loop(CX, smooth_rock, 8)
+    loop(CX, smooth_rock, UR)
     dots, halo_sent = iterate(0, rock_rhs, frac_rhs, send_faces(0), flux_sent)
+
     flux_sent = smooth_frac(1, W1F)
     dots += iterate(1, W1R, W1F, halo_sent, flux_sent)[0]
 
@@ -572,14 +578,13 @@
 
     def rock_update(i):
         rock_out[i] = on_b * (Z0[0, i + 1] + E[0, i + 1]) + on_p * (Z0[1, i + 1] + E[1, i + 1])
-    loop(CX, rock_update, 8)
+    loop(CX, rock_update, UR)
 
     def frac_update(r):
         frac_out[:, slab(r)] = on_b * ZF[0, :, slab(r)] + on_p * ZF[1, :, slab(r)]
-    loop(SLABS, frac_update, 8)
+    loop(SLABS, frac_update, UF)
     for copy in started:
         copy.wait_send()
-
 
 def local(sizes, rock_rhs, frac_rhs, perm, storage, pressure, frac_perm, frac_storage,
           frac_pressure, couple_geom, couple_count, couple_frac_cell, couple_rock_cell,
@@ -601,7 +606,7 @@
         mem(2, *tall), mem(2, *tall), mem(*tall), mem(*tall), mem(CX + 1, CY, NZ),
         *[mem(*block) for _ in range(9)], mem(ROWS, 128),
         *[mem(*frac) for _ in range(7)], mem(2, *frac), mem(FR * SLABS, 128), mem(FR * SLABS, 128),
-        mem(3, ROWS, FR * KC, kind=bf16), mem(3, 128, FR * KC, kind=bf16),
+        mem(3, ROWS, FR * KC, kind=bf16),
         mem(256, FR * KC, kind=bf16), mem(384, ROWS, kind=bf16), mem(256, FR * SLABS, kind=bf16),
         mem(FR, 128, 128, kind=bf16), mem(FR * SLABS, 2 * CROSS, kind=bf16),
         mem(256, 2 * CROSS, kind=bf16), mem(128, 4096, kind=bf16), mem(256, 4096, kind=bf16),
@@ -632,7 +637,6 @@
       cross_geom.reshape(1, CROSS), aggregates)
     return rock, fracs, norm[0, 0]
 
-
 def solution(mesh):
     n_gx, n_gy = mesh.shape["gx"], mesh.shape["gy"]
     n_z = 8 if n_gy % 8 == 0 else 2

time: 93.9 us -> 81.1 us (0.86)
  Pallas kernels: 88.9 us -> 76.1 us
    pallas_call x1, Pallas kernels: 88.9 us -> 76.1 us  [local(): pl.pallas_call(functools.partial(kernel, sizes), out_shape=(jax.ShapeDtyp...]
where the time goes in v2:
time: 81.1 us; the launch traced here: 81 us
  Pallas kernels  76.1 us (94%)
  local copies, waits for them, and re-layouts  2.52 us (3%)
  between operations  2.42 us (3%)
    pallas_call x1, Pallas kernels, local(): pl.pallas_call(functools.partial(kernel, sizes), out_shape=(jax.ShapeDtyp...  76.1 us
    unnamed x4, local copies, waits for them, and re-layouts  2.52 us

profile of v2, /device:TPU:1, one launch (start us, length us, event | category | flops | bytes accessed | tf_op | source)
XLA Modules:
  0.0 81.0 jit_solution(9742336179128788739)
XLA Ops:
  0.6 76.1 %shard_map.175 = (f32[32,16,128]{2,1,0:T(8,128)}, f32[32,4096]{1,0:T(8,128)}, f32[1,1]{1,0:T(1,128)}) custom-call(f32[32,16,128]{2,1,0:T(8,128)} %rock_rhs.1, f32[32,4096]{1,0:T(8,128)} %frac_rhs.1, f32[32,16,128]{2,1,0:T(8,128)} %perm.1, f32[32,16,128]{2,1,0:T(8,128)} %storage.1, f32[32,16,128]{2,1,0:T(8,128)} %pressure.1, f32[32,4096]{1,0:T(8,128)} %frac_perm.1, ...), custom_call_target="tpu_custom_call" | custom-call | tf_op jit(solution)/shard_map/pallas_call | solution.py:623
  76.7 0.0 copy-start
  76.7 1.7 %copy.22 = f32[32,16,128]{2,1,0:T(8,128)} copy(f32[32,16,128]{2,1,0:T(8,128)} %get-tuple-element.12) | data formatting | bytes 524288
  78.4 0.0 copy-done
  78.4 0.8 copy.23
Async XLA Ops:
  76.7 1.7 %copy-start = (f32[32,4096]{1,0:T(8,128)S(1)}, f32[32,4096]{1,0:T(8,128)}, u32[]{:S(2)}) copy-start(f32[32,4096]{1,0:T(8,128)} %get-tuple-element.13) | copy-start | bytes 1572868

commit v3 on v2

--- a/solution.py
+++ b/solution.py
@@ -20,37 +20,45 @@
 f32 = jnp.float32
 bf16 = jnp.bfloat16
 
+
 def iota(shape, dim):
     return lax.broadcasted_iota(jnp.int32, shape, dim)
 
+
 def loop(count, body, unroll=1):
     lax.fori_loop(0, count, lambda i, c: (body(i), c)[1], 0, unroll=unroll)
+
 
 def halves(x):
     high = x.astype(bf16)
     return high, (x - high.astype(f32)).astype(bf16)
 
+
 def nt_dot(a, b):
     return lax.dot_general(a, b, (((1,), (1,)), ((), ())), preferred_element_type=f32)
+
 
 def inverse(x):
     guess = pl.reciprocal(x, approx=True)
     guess = guess * (2.0 - x * guess)
     return guess * (2.0 - x * guess)
 
+
 def lanes_of(table, index):
     return jnp.take_along_axis(table, index, axis=1)
 
+
 def kernel(
     sizes,
-    rock_rhs, frac_rhs, perm, storage, pressure, frac_perm, frac_storage, frac_pressure,
-    geom, count, frac_cell, rock_cell, offset, pairs, cross_geom, agg,
+    rock_rhs_in, frac_rhs_in, perm_in, storage_in, pressure_in, frac_perm_in, frac_storage_in,
+    frac_pressure_in, geom, count, frac_cell, rock_cell, offset, pairs, cross_geom, agg_in,
     rock_out, frac_out, res_out,
     Z0, E, PA, PE, WX, WYM, WYP, WZM, WZP, RD, INVR, W1R, Q, S, DEL,
     FD, INVF, TAP, TAM, TCP, TCM, W1F, ZF, F2, S2,
     U, LV, TT, TF, BF, XU, LVX, AX, AY, AG, FI, XV, IDX, OFF, CPL, PICK, HV, AGS, VALS,
     sx, rx, sy, ry, sic, ric, szy, rzy, sfl, rfl, sans, rans, scs, rcs,
-    AR0, AR1, AR2, send_sem, recv_sem,
+    AR0, AR1, AR2, rock_rhs, frac_rhs, perm, storage, pressure, frac_perm, frac_storage,
+    frac_pressure, agg, send_sem, recv_sem, load_sem,
 ):
     n_gx, n_y, n_z = sizes
     n_gy = n_y * n_z
@@ -63,6 +71,16 @@
     y_peers = [(gx, (my_y + p) % n_y * n_z + my_z) for p in range(1, n_y)]
     z_peers = [(gx, my_y * n_z + (my_z + p) % n_z) for p in range(1, n_z)]
 
+    loads = [
+        pltpu.make_async_copy(src, dst, load_sem.at[n])
+        for n, (src, dst) in enumerate((
+            (frac_pressure_in, frac_pressure), (perm_in, perm), (pressure_in, pressure),
+            (agg_in, agg), (frac_perm_in, frac_perm), (frac_storage_in, frac_storage),
+            (frac_rhs_in, frac_rhs), (storage_in, storage), (rock_rhs_in, rock_rhs)))
+    ]
+    for copy in loads:
+        copy.start()
+
     barrier = pltpu.get_barrier_semaphore()
     everyone = gx_peers + y_peers + z_peers + y_dev
     for device in everyone:
@@ -166,20 +184,22 @@
             for m, part in enumerate((high, value - high)):
                 part = jnp.broadcast_to(part, (16, 128)).astype(bf16)
                 part = jnp.concatenate([part] * 8, axis=0)
-                LV[m * 128 : m * 128 + 128, slab(f)] = jnp.where(hot, part, bf16(0))
+                LV[src, m * 128 : m * 128 + 128, slab(f)] = jnp.where(hot, part, bf16(0))
         loop(FR, body, FR)
-        part = nt_dot(U[src], LV[...])
+        part = nt_dot(U[src], LV[src])
         total = part[:, :128] + part[:, 128:]
         DEL[...] = total if first else DEL[...] + total
 
-    def pick_rock(get, outs, agg_outs=None):
+    def turn_rock(get, with_agg):
         turn(get, 4, TT)
-        if agg_outs:
+        if with_agg:
             for m in range(4):
                 block = agg[m * 8 : m * 8 + 8].astype(f32).reshape(128, 128).T
                 TT[256:384, m * 128 : (m + 1) * 128] = block.astype(bf16)
+
+    def pick_rock(outs, agg_outs):
         table = TT[...] if agg_outs else TT[0:256]
-        for src in range(3):
+        for src in outs:
             got = jnp.dot(table, U[src], preferred_element_type=f32)
             for f in range(FR):
                 row, here = slice(f, f + 1), slice(f * 128, f * 128 + 128)
@@ -233,6 +253,7 @@
     def fold(x):
         return sum(x[j : j + 8] for j in range(0, x.shape[0], 8))
 
+    loads[0].wait()
     to_table(lambda r: frac_pressure[:, slab(r)])
     pick_slots(PICK)
 
@@ -251,6 +272,8 @@
     sic[0, 1] = CPL[...]
     sic[1, 1] = CPL[...]
 
+    for copy in loads[1:4]:
+        copy.wait()
     for d, plane in enumerate((CX - 1, 0)):
         sx[d, 0] = perm[plane]
         sx[d, 1] = pressure[plane]
@@ -264,6 +287,9 @@
     slots_sent = [send(sic.at[d], ric.at[d], y_dev[d]) for d in (0, 1)]
     faces_sent = [send(sx.at[d], rx.at[d], x_dev[d]) for d in (0, 1)]
     faces_sent += [send(sy.at[d], ry.at[d], y_dev[d]) for d in (0, 1)]
+
+    for copy in loads[4:]:
+        copy.wait()
 
     def scale_frac(r):
         press = frac_pressure[:, slab(r)]
@@ -297,7 +323,6 @@
     def build_lanes(f):
         BF[f] = (sub128 == (frac_cell[pl.ds(f, 1), :] & 127)).astype(f32).astype(bf16)
     loop(FR, build_lanes, 2)
-
     coefs = [XV[h : h + 1, :] for h in (0, 1)]
     spread_ends(coefs + coefs)
     spread_slots(CPL)
@@ -328,18 +353,14 @@
     flux_sent = smooth_frac(0, frac_rhs)
 
     build_hot(0)
-
     spread_rock(0, CPL, True)
-
     for copy in slots_sent:
         copy.wait_recv()
     for d in (0, 1):
         IDX[1 + d] = ric[d, 0].astype(jnp.int32)
         build_hot(1 + d)
         spread_rock(1 + d, ric.at[d, 1], False)
-
     build_aggregates()
-
     for copy in faces_sent:
         copy.wait_recv()
     open_x = [gx > 0, gx < n_gx - 1]
@@ -403,7 +424,6 @@
             diag = diag - jnp.where(near == mine, face, 0.0)
         S[i] = diag
     loop(CX, rock_diagonal, UR)
-
     coarse_diag = aggregate_sums(S)
     inverse_coarse = 1.0 / jnp.where(lane16 < NAGG, coarse_diag, 1.0)
 
@@ -422,17 +442,16 @@
         ] + [send(szy.at[k, d], rzy.at[k, d], y_dev[d]) for d in (0, 1)]
 
     def iterate(k, rock_vec, frac_vec, halo_sent, flux_sent):
-
-        pick_rock(lambda m: Z0[k, m * 8 + 1 : m * 8 + 9].reshape(128, 128),
-                  [HV, sans.at[k, 0, 0], sans.at[k, 1, 0]],
-                  None if k else [AGS, sans.at[k, 0, 1], sans.at[k, 1, 1]])
+        turn_rock(lambda m: Z0[k, m * 8 + 1 : m * 8 + 9].reshape(128, 128), k == 0)
+        pick_rock({1: sans.at[k, 0, 0], 2: sans.at[k, 1, 0]},
+                  None if k else {1: sans.at[k, 0, 1], 2: sans.at[k, 1, 1]})
         parts = 1 if k else 2
         answers_sent = [
             send(sans.at[k, 1 - d, 0:parts], rans.at[k, d, 0:parts], y_dev[d]) for d in (0, 1)]
-
         spread_rock(0, sfl.at[k], True)
-        for d, copy in enumerate(flux_sent):
+        for copy in flux_sent:
             copy.wait_recv()
+        for d in (0, 1):
             spread_rock(1 + d, rfl.at[k, d], False)
         for copy in halo_sent:
             copy.wait_recv()
@@ -445,12 +464,12 @@
             Q[i] = image
             S[i] = rock_vec[i] - image
         loop(CX, residual, UR)
-
         coarse = aggregate_sums(S) * inverse_coarse
         scs[k] = coarse[0:8]
         coarse_sent = [send(scs.at[k], rcs.at[k, d], x_dev[d]) for d in (0, 1)]
         coarse_sent += [send(scs.at[k], rcs.at[k, 2 + d], y_dev[d]) for d in (0, 1)]
 
+        pick_rock({0: HV}, None if k else {0: AGS})
         values = pick_ends()
         coefs = [XV[h : h + 1, :] for h in (0, 1)]
         spread_ends([coefs[h] * values[2 * (1 - e) + h] for e, h in ends])
@@ -472,7 +491,6 @@
             image = image - TCP[:, here] * down - TCM[:, here] * up
             FI[:, here] = image - relaxation * frac_vec[:, here]
         loop(SLABS, frac_faces, UF)
-
         for copy in answers_sent + coarse_sent:
             copy.wait_recv()
         if k == 0:
@@ -510,7 +528,6 @@
             return tuple(a + p for a, p in zip(accs, products(image, vec, rock_rhs[i])))
         accs = lax.fori_loop(0, CX, rock_image, (zero,) * 3, unroll=UR)
         halo_sent = send_faces(1) if k == 0 else None
-
         spread_slots(VALS.at[2])
 
         def frac_image(r, accs):
@@ -527,7 +544,6 @@
         Z0[0, i + 1] = rock_rhs[i] * INVR[i]
     loop(CX, smooth_rock, UR)
     dots, halo_sent = iterate(0, rock_rhs, frac_rhs, send_faces(0), flux_sent)
-
     flux_sent = smooth_frac(1, W1F)
     dots += iterate(1, W1R, W1F, halo_sent, flux_sent)[0]
 
@@ -586,13 +602,15 @@
     for copy in started:
         copy.wait_send()
 
+
 def local(sizes, rock_rhs, frac_rhs, perm, storage, pressure, frac_perm, frac_storage,
           frac_pressure, couple_geom, couple_count, couple_frac_cell, couple_rock_cell,
           host_offset, cross_pairs, cross_geom, aggregates):
     n_gx, n_y, n_z = sizes
     vmem = pl.BlockSpec(memory_space=pltpu.VMEM)
     smem = pl.BlockSpec(memory_space=pltpu.SMEM)
-    in_specs = [vmem] * 16
+    in_specs = [pl.BlockSpec(memory_space=pl.ANY)] * 8 + [vmem] * 7
+    in_specs.append(pl.BlockSpec(memory_space=pl.ANY))
     in_specs[9] = in_specs[12] = smem
     block = (CX, CY, NZ)
     tall = (CX + 2, CY, NZ)
@@ -607,7 +625,7 @@
         *[mem(*block) for _ in range(9)], mem(ROWS, 128),
         *[mem(*frac) for _ in range(7)], mem(2, *frac), mem(FR * SLABS, 128), mem(FR * SLABS, 128),
         mem(3, ROWS, FR * KC, kind=bf16),
-        mem(256, FR * KC, kind=bf16), mem(384, ROWS, kind=bf16), mem(256, FR * SLABS, kind=bf16),
+        mem(3, 256, FR * KC, kind=bf16), mem(384, ROWS, kind=bf16), mem(256, FR * SLABS, kind=bf16),
         mem(FR, 128, 128, kind=bf16), mem(FR * SLABS, 2 * CROSS, kind=bf16),
         mem(256, 2 * CROSS, kind=bf16), mem(128, 4096, kind=bf16), mem(256, 4096, kind=bf16),
         mem(256, 128, kind=bf16), mem(*frac), mem(8, 128),
@@ -618,7 +636,10 @@
         mem(2, 2, CX, NZ), mem(2, 2, CX, NZ), mem(2, *slot), mem(2, 2, *slot),
         mem(2, 2, 2, *slot), mem(2, 2, 2, *slot), mem(2, 8, 128), mem(2, 4, 8, 128),
         mem(n_gx, 8, 128), mem(n_y, 8, 128), mem(n_z, 8, 128),
+        mem(*block), mem(*frac), mem(*block), mem(*block), mem(*block), mem(*frac), mem(*frac),
+        mem(*frac), mem(*block, kind=jnp.int32),
         pltpu.SemaphoreType.DMA((64,)), pltpu.SemaphoreType.DMA((64,)),
+        pltpu.SemaphoreType.DMA((9,)),
     ]
     rock, fracs, norm = pl.pallas_call(
         functools.partial(kernel, sizes),
@@ -637,6 +658,7 @@
       cross_geom.reshape(1, CROSS), aggregates)
     return rock, fracs, norm[0, 0]
 
+
 def solution(mesh):
     n_gx, n_gy = mesh.shape["gx"], mesh.shape["gy"]
     n_z = 8 if n_gy % 8 == 0 else 2

time: 81.1 us -> 73.1 us (0.901)
  Pallas kernels: 76.1 us -> 68 us
    pallas_call x1, Pallas kernels: 76.1 us -> 68 us  [local(): pl.pallas_call(functools.partial(kernel, sizes), out_shape=(jax.ShapeDtyp...]
where the time goes in v3:
time: 73.1 us; the launch traced here: 72.9 us
  Pallas kernels  68 us (93%)
  local copies, waits for them, and re-layouts  2.52 us (3%)
  between operations  2.42 us (3%)
    pallas_call x1, Pallas kernels, local(): pl.pallas_call(functools.partial(kernel, sizes), out_shape=(jax.ShapeDtyp...  68 us
    unnamed x4, local copies, waits for them, and re-layouts  2.52 us

profile of v3, /device:TPU:1, one launch (start us, length us, event | category | flops | bytes accessed | tf_op | source)
XLA Modules:
  0.0 72.9 jit_solution(16724224138102662429)
XLA Ops:
  0.6 68.0 %shard_map.175 = (f32[32,16,128]{2,1,0:T(8,128)}, f32[32,4096]{1,0:T(8,128)}, f32[1,1]{1,0:T(1,128)}) custom-call(f32[32,16,128]{2,1,0:T(8,128)} %rock_rhs_in.1, f32[32,4096]{1,0:T(8,128)} %frac_rhs_in.1, f32[32,16,128]{2,1,0:T(8,128)} %perm_in.1, f32[32,16,128]{2,1,0:T(8,128)} %storage_in.1, f32[32,16,128]{2,1,0:T(8,128)} %pressure_in.1, ...), custom_call_target="tpu_custom_call" | custom-call | tf_op jit(solution)/shard_map/pallas_call | solution.py:644
  68.6 0.0 copy-start
  68.6 1.7 %copy.22 = f32[32,16,128]{2,1,0:T(8,128)} copy(f32[32,16,128]{2,1,0:T(8,128)} %get-tuple-element.12) | data formatting | bytes 524288
  70.4 0.0 copy-done
  70.4 0.8 %copy.23 = f32[32,4096]{1,0:T(8,128)} copy(f32[32,4096]{1,0:T(8,128)S(1)} %copy-done) | data formatting | bytes 1048576
Async XLA Ops:
  68.6 1.7 %copy-start = (f32[32,4096]{1,0:T(8,128)S(1)}, f32[32,4096]{1,0:T(8,128)}, u32[]{:S(2)}) copy-start(f32[32,4096]{1,0:T(8,128)} %get-tuple-element.13) | copy-start | bytes 1572868

commit v4 on v3

--- a/solution.py
+++ b/solution.py
@@ -477,6 +477,14 @@
         def correct(i):
             E[k, i + 1] = lanes_of(coarse, agg[i])
         loop(CX, correct, UR)
+        for plane in (0, CX + 1):
+            E[k, plane] = jnp.zeros((CY, NZ), f32)
+
+        def correct_image(i):
+            edge = jnp.zeros((1, NZ), f32)
+            image = stencil(i, E[k, i + 1], E[k, i], E[k, i + 2], edge, edge)
+            Q[i] = Q[i] + image - relaxation * rock_vec[i]
+        loop(CX, correct_image, UR)
 
         def frac_faces(r):
             here = slab(r)
@@ -496,8 +504,9 @@
         if k == 0:
             AGS[...] = AGS[...] + rans[0, 0, 1] + rans[0, 1, 1]
         tables = [jnp.concatenate([rcs[k, d], rcs[k, d]], axis=0) for d in range(4)]
-        for d, plane in enumerate((0, CX + 1)):
-            E[k, plane] = lanes_of(tables[d], rx[d, 2].astype(jnp.int32))
+        for d, plane in enumerate((0, CX - 1)):
+            near = lanes_of(tables[d], rx[d, 2].astype(jnp.int32))
+            Q[plane] = Q[plane] - WX[plane + d] * near
         for d in (0, 1):
             table = jnp.concatenate([tables[2 + d]] * 2, axis=0)
             VALS[d] = lanes_of(table, ry[d, 2].astype(jnp.int32))
@@ -516,18 +525,6 @@
                 return fold(v * v), fold(x * v), fold(x * x)
             return fold(x * b), fold(x * v), fold(x * x)
 
-        def rock_image(i, accs):
-            row = pl.ds(i, 1)
-            vec = rock_vec[i]
-            image = Q[i] + stencil(i, E[k, i + 1], E[k, i], E[k, i + 2],
-                                   VALS[0, row, :], VALS[1, row, :])
-            image = image - relaxation * vec
-            if k == 0:
-                W1R[i] = image
-                Z0[1, i + 1] = image * INVR[i]
-            return tuple(a + p for a, p in zip(accs, products(image, vec, rock_rhs[i])))
-        accs = lax.fori_loop(0, CX, rock_image, (zero,) * 3, unroll=UR)
-        halo_sent = send_faces(1) if k == 0 else None
         spread_slots(VALS.at[2])
 
         def frac_image(r, accs):
@@ -537,14 +534,26 @@
             if k == 0:
                 W1F[:, here] = image
             return tuple(a + p for a, p in zip(accs, products(image, vec, frac_rhs[:, here])))
-        accs = lax.fori_loop(0, SLABS, frac_image, accs, unroll=UF)
-        return list(accs), halo_sent
+        accs = lax.fori_loop(0, SLABS, frac_image, (zero,) * 3, unroll=UF)
+        flux_next = smooth_frac(1, W1F) if k == 0 else None
+
+        def rock_image(i, accs):
+            row = pl.ds(i, 1)
+            vec = rock_vec[i]
+            image = Q[i] - jnp.where(sub16 == 0, WYM[i] * VALS[0, row, :], 0.0)
+            image = image - jnp.where(sub16 == CY - 1, WYP[i] * VALS[1, row, :], 0.0)
+            if k == 0:
+                W1R[i] = image
+                Z0[1, i + 1] = image * INVR[i]
+            return tuple(a + p for a, p in zip(accs, products(image, vec, rock_rhs[i])))
+        accs = lax.fori_loop(0, CX, rock_image, accs, unroll=UR)
+        halo_next = send_faces(1) if k == 0 else None
+        return list(accs), halo_next, flux_next
 
     def smooth_rock(i):
         Z0[0, i + 1] = rock_rhs[i] * INVR[i]
     loop(CX, smooth_rock, UR)
-    dots, halo_sent = iterate(0, rock_rhs, frac_rhs, send_faces(0), flux_sent)
-    flux_sent = smooth_frac(1, W1F)
+    dots, halo_sent, flux_sent = iterate(0, rock_rhs, frac_rhs, send_faces(0), flux_sent)
     dots += iterate(1, W1R, W1F, halo_sent, flux_sent)[0]
 
     tile = jnp.zeros((8, 128), f32)
@@ -553,7 +562,16 @@
     groups = [(AR0, gx, gx_peers, n_gx), (AR1, my_y, y_peers, n_y), (AR2, my_z, z_peers, n_z)]
     for slots, me, peers, size in groups:
         slots[pl.ds(me, 1)] = tile[None]
+        earlier = len(started)
         copies = [send(slots.at[me], slots.at[me], device) for device in peers]
+        if slots is AR0:
+            def join(i):
+                for k in (0, 1):
+                    E[k, i + 1] = E[k, i + 1] + Z0[k, i + 1]
+            loop(CX, join, UR)
+        if slots is AR2:
+            for copy in started[:earlier]:
+                copy.wait_send()
         for copy in copies:
             copy.wait_recv()
         tile = sum(slots[n] for n in range(size))
@@ -593,13 +611,13 @@
     on_p = y1 * v1[1]
 
     def rock_update(i):
-        rock_out[i] = on_b * (Z0[0, i + 1] + E[0, i + 1]) + on_p * (Z0[1, i + 1] + E[1, i + 1])
+        rock_out[i] = on_b * E[0, i + 1] + on_p * E[1, i + 1]
     loop(CX, rock_update, UR)
 
     def frac_update(r):
         frac_out[:, slab(r)] = on_b * ZF[0, :, slab(r)] + on_p * ZF[1, :, slab(r)]
     loop(SLABS, frac_update, UF)
-    for copy in started:
+    for copy in started[earlier:]:
         copy.wait_send()
 
 

time: 73.1 us -> 72.7 us (level)
  no operation moved by 1% of the time
where the time goes in v4:
time: 72.7 us; the launch traced here: 72.5 us
  Pallas kernels  67.6 us (93%)
  local copies, waits for them, and re-layouts  2.52 us (3%)
  between operations  2.42 us (3%)
    pallas_call x1, Pallas kernels, local(): pl.pallas_call(functools.partial(kernel, sizes), out_shape=(jax.ShapeDtyp...  67.6 us
    unnamed x4, local copies, waits for them, and re-layouts  2.52 us

profile of v4, /device:TPU:1, one launch (start us, length us, event | category | flops | bytes accessed | tf_op | source)
XLA Modules:
  0.0 72.5 jit_solution(11088701871735688385)
XLA Ops:
  0.6 67.6 %shard_map.175 = (f32[32,16,128]{2,1,0:T(8,128)}, f32[32,4096]{1,0:T(8,128)}, f32[1,1]{1,0:T(1,128)}) custom-call(f32[32,16,128]{2,1,0:T(8,128)} %rock_rhs_in.1, f32[32,4096]{1,0:T(8,128)} %frac_rhs_in.1, f32[32,16,128]{2,1,0:T(8,128)} %perm_in.1, f32[32,16,128]{2,1,0:T(8,128)} %storage_in.1, f32[32,16,128]{2,1,0:T(8,128)} %pressure_in.1, ...), custom_call_target="tpu_custom_call" | custom-call | tf_op jit(solution)/shard_map/pallas_call | solution.py:662
  68.2 0.0 copy-start
  68.2 1.7 %copy.22 = f32[32,16,128]{2,1,0:T(8,128)} copy(f32[32,16,128]{2,1,0:T(8,128)} %get-tuple-element.12) | data formatting | bytes 524288
  70.0 0.0 copy-done
  70.0 0.8 %copy.23 = f32[32,4096]{1,0:T(8,128)} copy(f32[32,4096]{1,0:T(8,128)S(1)} %copy-done) | data formatting | bytes 1048576
Async XLA Ops:
  68.2 1.7 %copy-start = (f32[32,4096]{1,0:T(8,128)S(1)}, f32[32,4096]{1,0:T(8,128)}, u32[]{:S(2)}) copy-start(f32[32,4096]{1,0:T(8,128)} %get-tuple-element.13) | copy-start | bytes 1572868

commit v5 on v4

--- a/solution.py
+++ b/solution.py
@@ -57,7 +57,7 @@
     FD, INVF, TAP, TAM, TCP, TCM, W1F, ZF, F2, S2,
     U, LV, TT, TF, BF, XU, LVX, AX, AY, AG, FI, XV, IDX, OFF, CPL, PICK, HV, AGS, VALS,
     sx, rx, sy, ry, sic, ric, szy, rzy, sfl, rfl, sans, rans, scs, rcs,
-    AR0, AR1, AR2, rock_rhs, frac_rhs, perm, storage, pressure, frac_perm, frac_storage,
+    AR0, AR2, rock_rhs, frac_rhs, perm, storage, pressure, frac_perm, frac_storage,
     frac_pressure, agg, send_sem, recv_sem, load_sem,
 ):
     n_gx, n_y, n_z = sizes
@@ -67,8 +67,9 @@
     my_y, my_z = gy // n_z, gy % n_z
     x_dev = [((gx + 1) % n_gx, gy), ((gx + n_gx - 1) % n_gx, gy)]
     y_dev = [(gx, (gy + 1) % n_gy), (gx, (gy + n_gy - 1) % n_gy)]
-    gx_peers = [((gx + p) % n_gx, gy) for p in range(1, n_gx)]
-    y_peers = [(gx, (my_y + p) % n_y * n_z + my_z) for p in range(1, n_y)]
+    my_xy, n_xy = gx * n_y + my_y, n_gx * n_y
+    xy_peers = [
+        (n // n_y, n % n_y * n_z + my_z) for n in ((my_xy + p) % n_xy for p in range(1, n_xy))]
     z_peers = [(gx, my_y * n_z + (my_z + p) % n_z) for p in range(1, n_z)]
 
     loads = [
@@ -82,7 +83,7 @@
         copy.start()
 
     barrier = pltpu.get_barrier_semaphore()
-    everyone = gx_peers + y_peers + z_peers + y_dev
+    everyone = xy_peers + z_peers + y_dev
     for device in everyone:
         pl.semaphore_signal(barrier, inc=1, device_id=device, device_id_type=MESH)
 
@@ -559,7 +560,7 @@
     tile = jnp.zeros((8, 128), f32)
     for n, part in enumerate(dots):
         tile = jnp.where(sub8 == n, jnp.sum(part, axis=0, keepdims=True), tile)
-    groups = [(AR0, gx, gx_peers, n_gx), (AR1, my_y, y_peers, n_y), (AR2, my_z, z_peers, n_z)]
+    groups = [(AR0, my_xy, xy_peers, n_xy), (AR2, my_z, z_peers, n_z)]
     for slots, me, peers, size in groups:
         slots[pl.ds(me, 1)] = tile[None]
         earlier = len(started)
@@ -653,10 +654,10 @@
         mem(2, 2, *slot), mem(2, 2, *slot),
         mem(2, 2, CX, NZ), mem(2, 2, CX, NZ), mem(2, *slot), mem(2, 2, *slot),
         mem(2, 2, 2, *slot), mem(2, 2, 2, *slot), mem(2, 8, 128), mem(2, 4, 8, 128),
-        mem(n_gx, 8, 128), mem(n_y, 8, 128), mem(n_z, 8, 128),
+        mem(n_gx * n_y, 8, 128), mem(n_z, 8, 128),
         mem(*block), mem(*frac), mem(*block), mem(*block), mem(*block), mem(*frac), mem(*frac),
         mem(*frac), mem(*block, kind=jnp.int32),
-        pltpu.SemaphoreType.DMA((64,)), pltpu.SemaphoreType.DMA((64,)),
+        pltpu.SemaphoreType.DMA((80,)), pltpu.SemaphoreType.DMA((80,)),
         pltpu.SemaphoreType.DMA((9,)),
     ]
     rock, fracs, norm = pl.pallas_call(

time: 72.7 us -> 72.5 us (level)
  no operation moved by 1% of the time
where the time goes in v5:
time: 72.5 us; the launch traced here: 72.3 us
  Pallas kernels  67.4 us (93%)
  local copies, waits for them, and re-layouts  2.52 us (3%)
  between operations  2.42 us (3%)
    pallas_call x1, Pallas kernels, local(): pl.pallas_call(functools.partial(kernel, sizes), out_shape=(jax.ShapeDtyp...  67.4 us
    unnamed x4, local copies, waits for them, and re-layouts  2.52 us

profile of v5, /device:TPU:1, one launch (start us, length us, event | category | flops | bytes accessed | tf_op | source)
XLA Modules:
  0.0 72.3 jit_solution(15020555683002728005)
XLA Ops:
  0.6 67.4 %shard_map.175 = (f32[32,16,128]{2,1,0:T(8,128)}, f32[32,4096]{1,0:T(8,128)}, f32[1,1]{1,0:T(1,128)}) custom-call(f32[32,16,128]{2,1,0:T(8,128)} %rock_rhs_in.1, f32[32,4096]{1,0:T(8,128)} %frac_rhs_in.1, f32[32,16,128]{2,1,0:T(8,128)} %perm_in.1, f32[32,16,128]{2,1,0:T(8,128)} %storage_in.1, f32[32,16,128]{2,1,0:T(8,128)} %pressure_in.1, ...), custom_call_target="tpu_custom_call" | custom-call | tf_op jit(solution)/shard_map/pallas_call | solution.py:663
  68.0 0.0 copy-start
  68.0 1.7 %copy.22 = f32[32,16,128]{2,1,0:T(8,128)} copy(f32[32,16,128]{2,1,0:T(8,128)} %get-tuple-element.12) | data formatting | bytes 524288
  69.8 0.0 copy-done
  69.8 0.8 %copy.23 = f32[32,4096]{1,0:T(8,128)} copy(f32[32,4096]{1,0:T(8,128)S(1)} %copy-done) | data formatting | bytes 1048576
Async XLA Ops:
  68.0 1.7 %copy-start = (f32[32,4096]{1,0:T(8,128)S(1)}, f32[32,4096]{1,0:T(8,128)}, u32[]{:S(2)}) copy-start(f32[32,4096]{1,0:T(8,128)} %get-tuple-element.13) | copy-start | bytes 1572868
